TPU v7x, 32 devices: a whole 2x2x4 slice. The times are simulated.
32 devices in a mesh: sect: 2 (over core), cols: 16 (over z, y, x).
Axes of the slice: x: 2, y: 2, z: 4, core: 2. Of those that a mesh axis runs over, the one named last changes fastest.
Arguments:
- air_state: float32 [64, 6, 98304], P('sect', None, 'cols'), may hold values from -6 to 6
- mix_coef: float32 [64, 98304], P('sect', 'cols'), may hold values from 0.1 to 1600
- flux_scale: float32 [98304], P('cols'), may hold values from 0.5 to 4
- sea_state: float32 [6, 98304], P(None, ('sect', 'cols')), may hold values from -6 to 6
- sea_rate: float32 [98304], P(('sect', 'cols')), may hold values from 0.5 to 4
- block_counts: int32 [32, 48], P(('sect', 'cols')), may hold values from 1 to 256, 9830 in all within a row
- cell_column: int32 [393216], P(('sect', 'cols')), may hold values from 0 to 127
- cell_owner: int32 [393216, 1], P(('sect', 'cols')), may hold values from 0 to 31; in each aligned block of 12288 rows (0 to 12287, 12288 to 24575, ...) at most 480 rows name the same one
- cell_coef: float32 [393216], P(('sect', 'cols')), may hold values from 0.3 to 3
- cell_weight: float32 [393216], P(('sect', 'cols')), may hold values from 0.1 to 0.5
- slot_cell: int32 [491520], P(('sect', 'cols')), may hold values from 0 to 3071
- slot_frac: float32 [491520], P(('sect', 'cols')), may hold values from 0.2 to 1
Outputs:
- air_new: float32 [64, 6, 98304], P('sect', None, 'cols')
- sea_new: float32 [6, 98304], P(None, ('sect', 'cols'))
Inputs may be any that keep to these rules, and one draw needn't show every extreme that they name: `cell_owner`: among the slots of one device (aligned blocks of 12288 rows) no surface device is named more than 480 times, and some surface device exactly 480 times. `block_counts`: each device's counts have the same sum, and one block of every device is full.
All inputs are finite; a program needn't handle non-finite values.
Results may differ from a plain program's by a relative error of at most 0.0003.
Values sent between devices are 32-bit elements; how exact they have to be, the bound alone decides.
A program may use at most 128 MiB of HBM per device.

v0:
```python
import functools

import jax
import jax.numpy as jnp
from jax import lax
from jax.experimental import pallas as pl
from jax.experimental.pallas import tpu as pltpu
from jax.sharding import PartitionSpec as P

BLOCK_COLS = 128
BLOCK_SLOTS = 256
SUBSTEPS = 2
LANES = 128
COL_TILE = 1024
PARAMS = pltpu.CompilerParams(vmem_limit_bytes=40 * 1024 * 1024)


def split(value):
    high = value.astype(jnp.bfloat16).astype(jnp.float32)
    return high, value - high


def pair(ref, i):
    return jnp.concatenate([ref[pl.ds(2 * i, 1), :], ref[pl.ds(2 * i + 1, 1), :]], axis=1)


def onehot(index, count):
    return lax.broadcasted_iota(jnp.int32, (count, index.shape[1]), 0) == index


def lanes_map(lane):
    return jnp.where(onehot(lane, LANES), 1.0, 0.0).astype(jnp.bfloat16)


def spread(mask, values):
    values = values.astype(jnp.bfloat16)
    return jnp.concatenate([mask * values[q : q + 1] for q in range(values.shape[0])], axis=0)


def one_hot(index, count):
    return jnp.where(onehot(index, count), 1.0, 0.0).astype(jnp.bfloat16)


def scatter_step(acc, values, row, lane, rows):
    mask = one_hot(row, rows)
    high, low = split(values)
    lane_hot = lanes_map(lane)
    acc[...] += lax.dot_general(
        jnp.concatenate([spread(mask, high), spread(mask, low)], axis=1),
        jnp.concatenate([lane_hot, lane_hot], axis=1),
        (((1,), (1,)), ((), ())),
        preferred_element_type=jnp.float32,
    )


def table_of(value):
    high, low = split(value)
    return jnp.concatenate([high, low], axis=1).astype(jnp.bfloat16)


def gather_step(table, row, lane, rows, count):
    lane_hot = lanes_map(lane)
    picked = jnp.dot(
        table, jnp.concatenate([lane_hot, lane_hot], axis=0), preferred_element_type=jnp.float32
    )
    mask = onehot(row, rows)
    return jnp.concatenate(
        [
            jnp.sum(jnp.where(mask, picked[q * rows : (q + 1) * rows], 0.0), axis=0, keepdims=True)
            for q in range(count)
        ],
        axis=0,
    )


def setup_kernel(devices, cap_rows, owner, column, coef, weight, counts, out, acc, offset):
    acc[...] = jnp.zeros_like(acc)
    offset[...] = jnp.zeros_like(offset)
    later = (
        lax.broadcasted_iota(jnp.int32, (BLOCK_SLOTS, BLOCK_SLOTS), 0)
        <= lax.broadcasted_iota(jnp.int32, (BLOCK_SLOTS, BLOCK_SLOTS), 1)
    )
    later = jnp.where(later, 1.0, 0.0).astype(jnp.bfloat16)
    within = lax.broadcasted_iota(jnp.int32, (1, BLOCK_SLOTS), 1)

    def block(i, _):
        own = pair(owner, i)
        named = jnp.where(onehot(own, devices), 1.0, 0.0)
        running = (
            jnp.dot(named.astype(jnp.bfloat16), later, preferred_element_type=jnp.float32)
            + offset[:, 0:1]
        )
        rank = (jnp.sum(named * running, axis=0, keepdims=True) - 1.0).astype(jnp.int32)
        offset[...] += jnp.broadcast_to(jnp.sum(named, axis=1, keepdims=True), offset.shape)
        live = within < counts[pl.ds(i, 1), 0:1]
        gain = jnp.where(live, pair(coef, i), 0.0)
        flow = pair(weight, i) * gain
        gain_high, gain_low = split(gain)
        flow_high, flow_low = split(flow)
        values = jnp.concatenate(
            [
                jnp.full((1, BLOCK_SLOTS), i, jnp.int32).astype(jnp.float32),
                pair(column, i).astype(jnp.float32),
                gain_high,
                gain_low,
                flow_high,
                flow_low,
            ],
            axis=0,
        )
        acc[...] += lax.dot_general(
            spread(one_hot(own * cap_rows + rank // LANES, LANES), values),
            lanes_map(rank % LANES),
            (((1,), (1,)), ((), ())),
            preferred_element_type=jnp.float32,
        )
        return 0

    lax.fori_loop(0, owner.shape[0] // 2, block, 0, unroll=4)
    out[0] = acc[0:128]
    out[1] = acc[128:256]
    out[2] = acc[256:384] + acc[384:512]
    out[3] = acc[512:640] + acc[640:768]


def setup(owner, column, coef, weight, counts, devices, cap_rows):
    return pl.pallas_call(
        functools.partial(setup_kernel, devices, cap_rows),
        out_shape=jax.ShapeDtypeStruct((4, LANES, LANES), jnp.float32),
        scratch_shapes=[
            pltpu.VMEM((6 * LANES, LANES), jnp.float32),
            pltpu.VMEM((devices, LANES), jnp.float32),
        ],
        compiler_params=PARAMS,
    )(owner, column, coef, weight, counts)


def level_down(mix, air, k, under, carried):
    coupling = mix[k : k + 1, :]
    inverse = 1.0 / (1.0 + coupling + under)
    part = (air[k] + carried) * inverse
    ratio = coupling * inverse
    return part, ratio, inverse, ratio * (1.0 + under), coupling * part


def descend_end_kernel(air, mix, end):
    under = jnp.zeros((1, end.shape[1]), jnp.float32)
    carried = jnp.zeros((air.shape[0], end.shape[1]), jnp.float32)
    levels_first = jnp.swapaxes(air[...], 0, 1)
    for k in range(air.shape[1]):
        _, _, _, under, carried = level_down(mix, levels_first, k, under, carried)
    end[...] = jnp.concatenate([carried, under], axis=0)


def descend_end(air, mix):
    tracers, levels, columns = air.shape
    return pl.pallas_call(
        descend_end_kernel,
        grid=(columns // COL_TILE,),
        in_specs=[
            pl.BlockSpec((tracers, levels, COL_TILE), lambda j: (0, 0, j)),
            pl.BlockSpec((levels, COL_TILE), lambda j: (0, j)),
        ],
        out_specs=pl.BlockSpec((tracers + 1, COL_TILE), lambda j: (0, j)),
        out_shape=jax.ShapeDtypeStruct((tracers + 1, columns), jnp.float32),
        compiler_params=PARAMS,
    )(air, mix)


def descend_kernel(air, mix, start, last, parts, ratios, ends):
    tracers, levels, _ = air.shape
    levels_first = jnp.swapaxes(air[...], 0, 1)
    carried = start[0:tracers, :]
    under = start[tracers : tracers + 1, :]
    for k in range(levels):
        part, ratio, inverse, under, carried = level_down(mix, levels_first, k, under, carried)
        parts[k] = part
        if k == levels - 1:
            ratio = last[...] * inverse
        ratios[k : k + 1, :] = ratio
    value, factor = part, ratio
    ends[0, 0:tracers, :] = part
    ends[0, tracers : tracers + 1, :] = ratio
    for k in range(levels - 2, -1, -1):
        ratio = ratios[k : k + 1, :]
        value = parts[k] + ratio * value
        factor = ratio * factor
    ends[1, 0:tracers, :] = value
    ends[1, tracers : tracers + 1, :] = factor


def descend(air, mix, start, last):
    tracers, levels, columns = air.shape
    return pl.pallas_call(
        descend_kernel,
        grid=(columns // COL_TILE,),
        in_specs=[
            pl.BlockSpec((tracers, levels, COL_TILE), lambda j: (0, 0, j)),
            pl.BlockSpec((levels, COL_TILE), lambda j: (0, j)),
            pl.BlockSpec((tracers + 1, COL_TILE), lambda j: (0, j)),
            pl.BlockSpec((1, COL_TILE), lambda j: (0, j)),
        ],
        out_specs=[
            pl.BlockSpec((levels, tracers, COL_TILE), lambda j: (0, 0, j)),
            pl.BlockSpec((levels, COL_TILE), lambda j: (0, j)),
            pl.BlockSpec((2, tracers + 1, COL_TILE), lambda j: (0, 0, j)),
        ],
        out_shape=[
            jax.ShapeDtypeStruct((levels, tracers, columns), jnp.float32),
            jax.ShapeDtypeStruct(mix.shape, jnp.float32),
            jax.ShapeDtypeStruct((2, tracers + 1, columns), jnp.float32),
        ],
        compiler_params=PARAMS,
    )(air, mix, start, last)


def ascend_kernel(parts, ratios, below, out):
    value = below[...]
    risen = []
    for k in range(parts.shape[0] - 1, -1, -1):
        value = parts[k] + ratios[k : k + 1, :] * value
        risen.append(value)
    out[...] = jnp.swapaxes(jnp.stack(risen[::-1]), 0, 1)


def ascend(parts, ratios, below):
    levels, tracers, columns = parts.shape
    return pl.pallas_call(
        ascend_kernel,
        grid=(columns // COL_TILE,),
        in_specs=[
            pl.BlockSpec((levels, tracers, COL_TILE), lambda j: (0, 0, j)),
            pl.BlockSpec((levels, COL_TILE), lambda j: (0, j)),
            pl.BlockSpec((tracers, COL_TILE), lambda j: (0, j)),
        ],
        out_specs=pl.BlockSpec((tracers, levels, COL_TILE), lambda j: (0, 0, j)),
        out_shape=jax.ShapeDtypeStruct((tracers, levels, columns), jnp.float32),
        compiler_params=PARAMS,
    )(parts, ratios, below)


def exchange_kernel(
    tracers,
    sections,
    ring,
    resid,
    slope,
    flux,
    other,
    block,
    column,
    flow,
    gain,
    frac,
    row,
    lane,
    sea,
    rate,
    flux_new,
    sea_new,
    sent,
    arrived,
    back,
    returned,
    acc,
    out_send,
    out_recv,
    back_send,
    back_recv,
):
    devices = sections * ring
    rows, surf_rows = slope.shape[0], rate.shape[0]
    parts = back.shape[1] // tracers
    acc_rows = acc.shape[0] // (tracers + 1)
    me = lax.axis_index("sect") * ring + lax.axis_index("cols")

    def coords(device):
        return (device // ring, lax.rem(device, ring))

    def ahead(s):
        return lax.rem(me + s, devices)

    def behind(s):
        return lax.rem(me + devices - s, devices)

    def outward(s):
        device = ahead(s)
        return pltpu.make_async_remote_copy(
            src_ref=sent.at[device],
            dst_ref=arrived.at[me],
            send_sem=out_send.at[s],
            recv_sem=out_recv.at[s],
            device_id=coords(device),
            device_id_type=pl.DeviceIdType.MESH,
        )

    def homeward(s):
        device = ahead(s)
        return pltpu.make_async_remote_copy(
            src_ref=back.at[device],
            dst_ref=returned.at[me],
            send_sem=back_send.at[s],
            recv_sem=back_recv.at[s],
            device_id=coords(device),
            device_id_type=pl.DeviceIdType.MESH,
        )

    def pack(values):
        return jnp.concatenate(
            [values[:, p * LANES : (p + 1) * LANES] for p in range(parts)], axis=0
        )

    def unpack(values):
        count = values.shape[0] // parts
        return jnp.concatenate([values[p * count : (p + 1) * count] for p in range(parts)], axis=1)

    def rows_of(ref, sources):
        return jnp.concatenate([ref[pl.ds(source, 1), :] for source in sources], axis=1)

    def in_pairs(act):
        act(1)

        def both(p, _):
            act(2 * p, 2 * p + 1)
            return 0

        lax.fori_loop(1, devices // 2, both, 0)

    barrier = pltpu.get_barrier_semaphore()

    def greet(s, _):
        pl.semaphore_signal(
            barrier,
            inc=1,
            device_id=coords(ahead(s)),
            device_id_type=pl.DeviceIdType.MESH,
        )
        return 0

    lax.fori_loop(1, devices, greet, 0)
    bottom = resid[...] + jnp.concatenate([slope[...]] * tracers, axis=0) * (flux[...] + other[...])
    table = table_of(bottom)

    def at_cells(device):
        here = pl.ds(device, 1)
        picked = gather_step(table, block[here, :], column[here, :], rows, tracers)
        return pack(jnp.concatenate([picked, gain[here, :]], axis=0))

    own = at_cells(me)
    sent[me] = own
    pl.semaphore_wait(barrier, devices - 1)

    def send(*steps):
        chunks = [at_cells(ahead(s)) for s in steps]
        for s, chunk in zip(steps, chunks):
            sent[ahead(s)] = chunk
        for s in steps:
            outward(s).start()

    in_pairs(send)
    acc[...] = jnp.zeros_like(acc)

    def add(chunks, sources):
        came = jnp.concatenate([unpack(chunk) for chunk in chunks], axis=1)
        strength = came[tracers:] * rows_of(frac, sources)
        scatter_step(
            acc,
            jnp.concatenate([came[0:tracers] * strength, strength], axis=0),
            rows_of(row, sources),
            rows_of(lane, sources),
            acc_rows,
        )

    add([own], [me])

    def receive(*steps):
        for s in steps:
            outward(s).wait_recv()
        add([arrived[behind(s)] for s in steps], [behind(s) for s in steps])

    in_pairs(receive)
    pace = rate[...]
    inverse = 1.0 / (1.0 + pace * acc[tracers * acc_rows : tracers * acc_rows + surf_rows])
    for q in range(tracers):
        here = slice(q * surf_rows, (q + 1) * surf_rows)
        summed = acc[q * acc_rows : q * acc_rows + surf_rows]
        sea_new[here] = (sea[here] + pace * summed) * inverse
    sea_table = table_of(sea_new[...])

    def seen(device):
        here = pl.ds(device, 1)
        return pack(gather_step(sea_table, row[here, :], lane[here, :], surf_rows, tracers))

    def give_back(*steps):
        chunks = [seen(ahead(s)) for s in steps]
        for s, chunk in zip(steps, chunks):
            back[ahead(s)] = chunk
        for s in steps:
            homeward(s).start()

    in_pairs(give_back)
    flux_new[...] = jnp.zeros_like(flux_new)

    def collect(chunks, sources):
        change = [
            unpack(chunk) - unpack(sent[source])[0:tracers]
            for chunk, source in zip(chunks, sources)
        ]
        scatter_step(
            flux_new,
            jnp.concatenate(change, axis=1) * rows_of(flow, sources),
            rows_of(block, sources),
            rows_of(column, sources),
            rows,
        )

    collect([seen(me)], [me])

    def take_back(*steps):
        for s in steps:
            homeward(s).wait_recv()
        collect([returned[behind(s)] for s in steps], [behind(s) for s in steps])

    in_pairs(take_back)

    def finish(s, _):
        outward(s).wait_send()
        homeward(s).wait_send()
        return 0

    lax.fori_loop(1, devices, finish, 0)


def exchange(tracers, sections, ring, resid, slope, flux, other, block, column, flow, *surface):
    devices, slots = block.shape
    surf_rows = surface[-1].shape[0]
    outgoing = pltpu.VMEM((devices, (tracers + 1) * slots // LANES, LANES), jnp.float32)
    homecoming = pltpu.VMEM((devices, tracers * slots // LANES, LANES), jnp.float32)
    return pl.pallas_call(
        functools.partial(exchange_kernel, tracers, sections, ring),
        out_shape=[
            jax.ShapeDtypeStruct(resid.shape, jnp.float32),
            jax.ShapeDtypeStruct((tracers * surf_rows, LANES), jnp.float32),
        ],
        in_specs=[pl.BlockSpec(memory_space=pltpu.VMEM)] * 13,
        out_specs=[pl.BlockSpec(memory_space=pltpu.VMEM)] * 2,
        scratch_shapes=[
            outgoing,
            outgoing,
            homecoming,
            homecoming,
            pltpu.VMEM(((tracers + 1) * (-(-surf_rows // 16) * 16), LANES), jnp.float32),
            pltpu.SemaphoreType.DMA((devices,)),
            pltpu.SemaphoreType.DMA((devices,)),
            pltpu.SemaphoreType.DMA((devices,)),
            pltpu.SemaphoreType.DMA((devices,)),
        ],
        compiler_params=pltpu.CompilerParams(
            vmem_limit_bytes=40 * 1024 * 1024, collective_id=0, has_side_effects=True
        ),
    )(resid, slope, flux, other, block, column, flow, *surface)


def body(
    air_state,
    mix_coef,
    flux_scale,
    sea_state,
    sea_rate,
    block_counts,
    cell_column,
    cell_owner,
    cell_coef,
    cell_weight,
    slot_cell,
    slot_frac,
):
    levels, tracers, columns = air_state.shape
    is_lower = lax.axis_index("sect") == 1
    devices = lax.axis_size("sect") * lax.axis_size("cols")
    rows = columns // BLOCK_COLS
    surf_cells = sea_state.shape[1]
    surf_rows = surf_cells // LANES
    capacity = slot_cell.shape[0] // devices
    cap_rows = -(-capacity // LANES)
    padding = ((0, 0), (0, cap_rows * LANES - capacity))

    air = jnp.swapaxes(air_state, 0, 1)
    handed = lax.ppermute(descend_end(air, mix_coef), "sect", [(0, 1)])
    slots = setup(
        cell_owner.reshape(-1, LANES),
        cell_column.reshape(-1, LANES),
        cell_coef.reshape(-1, LANES),
        cell_weight.reshape(-1, LANES),
        jnp.broadcast_to(block_counts.reshape(-1, 1), (rows, LANES)),
        devices,
        cap_rows,
    )
    slots = slots.reshape(4, LANES * LANES)[:, : devices * cap_rows * LANES]
    slots = slots.reshape(4, devices, cap_rows * LANES)
    block = slots[0].astype(jnp.int32)
    column = slots[1].astype(jnp.int32)
    cell = jnp.pad(slot_cell.reshape(devices, capacity), padding)
    frac = jnp.pad(slot_frac.reshape(devices, capacity), padding)
    row, lane = cell // LANES, cell % LANES

    last = jnp.where(is_lower, flux_scale, mix_coef[-1])[None]
    parts, ratios, ends = descend(air, mix_coef, handed, last)
    received = lax.ppermute(ends, "sect", [(1, 0)])
    low = jnp.where(is_lower, ends, received)
    resid = low[0, :tracers].reshape(tracers * rows, LANES)
    slope = low[0, tracers].reshape(rows, LANES)

    sea = sea_state.reshape(tracers * surf_rows, LANES)
    rate = sea_rate.reshape(surf_rows, LANES)
    flux = other = jnp.zeros((tracers * rows, LANES), jnp.float32)
    for _ in range(SUBSTEPS):
        flux, sea = exchange(
            tracers,
            lax.axis_size("sect"),
            lax.axis_size("cols"),
            resid,
            slope,
            flux,
            other,
            block,
            column,
            slots[3],
            slots[2],
            frac,
            row,
            lane,
            sea,
            rate,
        )
        other = lax.ppermute(flux, "sect", [(0, 1), (1, 0)])
    flux_col = (flux + other).reshape(tracers, columns)
    below = jnp.where(is_lower, flux_col, low[1, :tracers] + low[1, tracers] * flux_col)
    return (jnp.swapaxes(ascend(parts, ratios, below), 0, 1), sea.reshape(tracers, surf_cells))


def solution(mesh):
    return jax.shard_map(
        body,
        mesh=mesh,
        in_specs=(
            P("sect", None, "cols"),
            P("sect", "cols"),
            P("cols"),
            P(None, ("sect", "cols")),
            P(("sect", "cols")),
            P(("sect", "cols"), None),
            P(("sect", "cols")),
            P(("sect", "cols"), None),
            P(("sect", "cols")),
            P(("sect", "cols")),
            P(("sect", "cols")),
            P(("sect", "cols")),
        ),
        out_specs=(P("sect", None, "cols"), P(None, ("sect", "cols"))),
        check_vma=False,
    )
```

profile of v0, /device:TPU:0, one launch (start us, length us, event | category | flops | bytes accessed | tf_op | source)
XLA Modules:
  0.0 123.8 jit_solution(1873392087656431110)
XLA Ops:
  0.7 2.3 %copy-done = f32[32,6,6144]{2,0,1:T(8,128)S(1)} copy-done((f32[32,6,6144]{2,0,1:T(8,128)S(1)}, f32[32,6,6144]{2,0,1:T(8,128)}, u32[]{:S(2)}) %copy-start) | copy-done | bytes 4718616
  3.0 1.1 copy-done.4
  4.2 4.2 %shard_map.131 = f32[7,6144]{1,0:T(8,128)S(1)} custom-call(f32[6,32,6144]{2,1,0:T(8,128)S(1)} %bitcast.18, f32[32,6144]{1,0:T(8,128)S(1)} %copy-done.4), custom_call_target="tpu_custom_call" | custom-call | tf_op jit(solution)/shard_map/pallas_call | solution.py:157
  8.3 2.5 %collective-permute-start = (f32[7,6144]{1,0:T(8,128)S(1)}, f32[7,6144]{1,0:T(8,128)S(1)}, u32[]{:S(2)}, u32[]{:S(2)}) collective-permute-start(f32[7,6144]{1,0:T(8,128)S(1)} %shard_map.131), channel_id=1, source_target_pairs={{0,16},{1,17},{2,18},{3,19},{4,20},{5,21},{6,22},{7,23},{8,24},{9,... | collective-permute-start | bytes 516104 | tf_op jit(solution)/shard_map/ppermute | solution.py:489
  10.9 0.1 broadcast_in_dim.16.counts
  11.0 17.6 %shard_map.133 = f32[4,128,128]{2,1,0:T(8,128)S(1)} custom-call(s32[96,128]{1,0:T(8,128)S(1)} %bitcast.25, s32[96,128]{1,0:T(8,128)S(1)} %bitcast.26, f32[96,128]{1,0:T(8,128)S(1)} %bitcast.27, f32[96,128]{1,0:T(8,128)S(1)} %bitcast.28, s32[48,128]{1,0:T(8,128)S(1)} %broadcast_in_dim.16.counts), custom_call_target="tpu_custom_call" | custom-call | tf_op jit(solution)/shard_map/pallas_call | solution.py:127
  28.7 2.3 %copy-done.1 = f32[32,6,6144]{2,0,1:T(8,128)S(1)} copy-done((f32[32,6,6144]{2,0,1:T(8,128)S(1)}, f32[32,6,6144]{2,0,1:T(8,128)}, u32[]{:S(2)}) %copy-start.1) | copy-done | bytes 4718616
  31.0 5.2 %shard_map.132 = (f32[32,6,6144]{2,1,0:T(8,128)S(1)}, f32[32,6144]{1,0:T(8,128)S(1)}, f32[2,7,6144]{2,1,0:T(8,128)S(1)}) custom-call(f32[6,32,6144]{2,1,0:T(8,128)S(1)} %bitcast.19, f32[32,6144]{1,0:T(8,128)S(1)} %copy-done.5, f32[7,6144]{1,0:T(8,128)S(1)} %collective-permute-done.start, f32[1,6144]{1,0:T(1,128)S(1)} %bitcast.22), custom_call_target="tpu_custom_call" | custom-call | tf_op jit(solution)/shard_map/pallas_call | solution.py:194
  36.2 2.6 %copy-done.2 = f32[32,6,6144]{2,1,0:T(8,128)} copy-done((f32[32,6,6144]{2,1,0:T(8,128)}, f32[32,6,6144]{2,1,0:T(8,128)S(1)}, u32[]{:S(2)}) %copy-start.2) | copy-done | bytes 4718616
  38.9 1.3 %collective-permute-start.1 = (f32[2,7,6144]{2,1,0:T(8,128)S(1)}, f32[2,7,6144]{2,1,0:T(8,128)S(1)}, u32[]{:S(2)}, u32[]{:S(2)}) collective-permute-start(f32[2,7,6144]{2,1,0:T(8,128)S(1)} %get-tuple-element.11), channel_id=1, source_target_pairs={{16,0},{17,1},{18,2},{19,3},{20,4},{21,5},{22,6},{23,7},{24,8},{25... | collective-permute-start | bytes 1032200 | tf_op jit(solution)/shard_map/ppermute | solution.py:509
  40.3 0.1 reshape.52
  40.4 0.1 reshape.51
  40.5 0.1 add_select_fusion
  40.6 1.9 %collective-permute-done.1 = f32[2,7,6144]{2,1,0:T(8,128)S(1)} collective-permute-done((f32[2,7,6144]{2,1,0:T(8,128)S(1)}, f32[2,7,6144]{2,1,0:T(8,128)S(1)}, u32[]{:S(2)}, u32[]{:S(2)}) %collective-permute-start.1) | collective-permute-done | bytes 344096 | tf_op jit(solution)/shard_map/ppermute | solution.py:509
  42.5 0.1 broadcast_select_fusion
  42.7 36.2 %shard_map.134 = (f32[288,128]{1,0:T(8,128)S(1)}, f32[144,128]{1,0:T(8,128)S(1)}) custom-call(f32[288,128]{1,0:T(8,128)S(1)} %reshape_squeeze.6.resid, f32[48,128]{1,0:T(8,128)S(1)} %bitcast.20, f32[288,128]{1,0:T(8,128)S(1)} %broadcast_in_dim.14.flux.other, f32[288,128]{1,0:T(8,128)S(1)} %broadcast_in_dim.14.flux.other, ...), custom_call_target="tpu_custom_call" | custom-call | tf_op jit(solution)/shard_map/pallas_call | solution.py:439
  78.9 0.1 collective-permute-start.2
  79.0 1.4 %collective-permute-done.2.other = f32[288,128]{1,0:T(8,128)S(1)} collective-permute-done((f32[288,128]{1,0:T(8,128)S(1)}, f32[288,128]{1,0:T(8,128)S(1)}, u32[]{:S(2)}, u32[]{:S(2)}) %collective-permute-start.2) | collective-permute-done | bytes 147488 | tf_op jit(solution)/shard_map/ppermute | solution.py:536
  80.3 34.7 %shard_map.135 = (f32[288,128]{1,0:T(8,128)S(1)}, f32[144,128]{1,0:T(8,128)S(1)}) custom-call(f32[288,128]{1,0:T(8,128)S(1)} %reshape_squeeze.6.resid, f32[48,128]{1,0:T(8,128)S(1)} %bitcast.21, f32[288,128]{1,0:T(8,128)S(1)} %get-tuple-element.12.flux, f32[288,128]{1,0:T(8,128)S(1)} %collective-permute-done.2.other, ...), custom_call_target="tpu_custom_call" | custom-call | tf_op jit(solution)/shard_map/pallas_call | solution.py:439
  115.0 0.1 collective-permute-start.3
  115.1 0.7 reshape.56
  115.8 0.7 collective-permute-done.3
  116.6 2.8 %copy-done.3 = f32[32,6,6144]{2,1,0:T(8,128)S(1)} copy-done((f32[32,6,6144]{2,1,0:T(8,128)S(1)}, f32[32,6,6144]{2,1,0:T(8,128)}, u32[]{:S(2)}) %copy-start.3) | copy-done | bytes 4718616
  119.4 4.4 %shard_map.136 = f32[6,32,6144]{2,1,0:T(8,128)} custom-call(f32[32,6,6144]{2,1,0:T(8,128)S(1)} %copy-done.3, f32[32,6144]{1,0:T(8,128)S(1)} %get-tuple-element.10.ratios, f32[6,6144]{1,0:T(8,128)S(1)} %fusion.1.below), custom_call_target="tpu_custom_call" | custom-call | tf_op jit(solution)/shard_map/pallas_call | solution.py:228
  (44 shorter events, 0.4 us)
Async XLA Ops:
  0.6 10.3 %copy-start.15 = (s32[1,48]{1,0:T(1,128)S(1)}, s32[1,48]{1,0:T(1,128)}, u32[]{:S(2)}) copy-start(s32[1,48]{1,0:T(1,128)} %param.17) | copy-start | bytes 580
  0.6 2.3 %copy-start = (f32[32,6,6144]{2,0,1:T(8,128)S(1)}, f32[32,6,6144]{2,0,1:T(8,128)}, u32[]{:S(2)}) copy-start(f32[32,6,6144]{2,0,1:T(8,128)} %param.12) | copy-start | bytes 14155780
  3.0 1.1 copy-start.4
  4.1 6.9 %copy-start.7 = (s32[12288,1]{0,1:T(1,128)S(1)}, s32[12288,1]{0,1:T(1,128)}, u32[]{:S(2)}) copy-start(s32[12288,1]{0,1:T(1,128)} %param.19) | copy-start | bytes 147460
  4.1 6.9 %copy-start.8 = (s32[12288]{0:T(1024)S(1)}, s32[12288]{0:T(1024)}, u32[]{:S(2)}) copy-start(s32[12288]{0:T(1024)} %param.18) | copy-start | bytes 147460
  4.1 6.9 %copy-start.9 = (f32[12288]{0:T(1024)S(1)}, f32[12288]{0:T(1024)}, u32[]{:S(2)}) copy-start(f32[12288]{0:T(1024)} %param.20) | copy-start | bytes 147460
  4.1 6.9 %copy-start.10 = (f32[12288]{0:T(1024)S(1)}, f32[12288]{0:T(1024)}, u32[]{:S(2)}) copy-start(f32[12288]{0:T(1024)} %param.21) | copy-start | bytes 147460
  4.1 24.5 %copy-start.14 = (f32[6144]{0:T(1024)S(1)}, f32[6144]{0:T(1024)}, u32[]{:S(2)}) copy-start(f32[6144]{0:T(1024)} %param.14) | copy-start | bytes 73732
  4.1 24.5 %copy-start.5 = (f32[32,6144]{1,0:T(8,128)S(1)}, f32[32,6144]{1,0:T(8,128)}, u32[]{:S(2)}) copy-start(f32[32,6144]{1,0:T(8,128)} %mix.3) | copy-start | bytes 2359300
  8.3 32.0 %copy-start.12 = (s32[15360]{0:T(1024)S(1)}, s32[15360]{0:T(1024)}, u32[]{:S(2)}) copy-start(s32[15360]{0:T(1024)} %param.22) | copy-start | bytes 184324
  8.3 32.1 %copy-start.13 = (f32[15360]{0:T(1024)S(1)}, f32[15360]{0:T(1024)}, u32[]{:S(2)}) copy-start(f32[15360]{0:T(1024)} %param.23) | copy-start | bytes 184324
  8.3 32.2 %copy-start.11 = (f32[6,3072]{1,0:T(8,128)S(1)}, f32[6,3072]{1,0:T(8,128)}, u32[]{:S(2)}) copy-start(f32[6,3072]{1,0:T(8,128)} %param.15) | copy-start | bytes 221188
  8.3 20.3 %collective-permute-start = (f32[7,6144]{1,0:T(8,128)S(1)}, f32[7,6144]{1,0:T(8,128)S(1)}, u32[]{:S(2)}, u32[]{:S(2)}) collective-permute-start(f32[7,6144]{1,0:T(8,128)S(1)} %shard_map.131), channel_id=1, source_target_pairs={{0,16},{1,17},{2,18},{3,19},{4,20},{5,21},{6,22},{7,23},{8,24},{9,... | collective-permute-start | bytes 516104 | tf_op jit(solution)/shard_map/ppermute | solution.py:489
  28.7 2.3 %copy-start.1 = (f32[32,6,6144]{2,0,1:T(8,128)S(1)}, f32[32,6,6144]{2,0,1:T(8,128)}, u32[]{:S(2)}) copy-start(f32[32,6,6144]{2,0,1:T(8,128)} %param.12) | copy-start | bytes 14155780
  31.0 11.7 %copy-start.6 = (f32[3072]{0:T(1024)S(1)}, f32[3072]{0:T(1024)}, u32[]{:S(2)}) copy-start(f32[3072]{0:T(1024)} %param.16) | copy-start | bytes 36868
  36.2 2.7 %copy-start.2 = (f32[32,6,6144]{2,1,0:T(8,128)}, f32[32,6,6144]{2,1,0:T(8,128)S(1)}, u32[]{:S(2)}) copy-start(f32[32,6,6144]{2,1,0:T(8,128)S(1)} %get-tuple-element.9.parts) | copy-start | bytes 14155780
  38.9 3.6 %collective-permute-start.1 = (f32[2,7,6144]{2,1,0:T(8,128)S(1)}, f32[2,7,6144]{2,1,0:T(8,128)S(1)}, u32[]{:S(2)}, u32[]{:S(2)}) collective-permute-start(f32[2,7,6144]{2,1,0:T(8,128)S(1)} %get-tuple-element.11), channel_id=1, source_target_pairs={{16,0},{17,1},{18,2},{19,3},{20,4},{21,5},{22,6},{23,7},{24,8},{25... | collective-permute-start | bytes 1032200 | tf_op jit(solution)/shard_map/ppermute | solution.py:509
  78.9 1.4 %collective-permute-start.2 = (f32[288,128]{1,0:T(8,128)S(1)}, f32[288,128]{1,0:T(8,128)S(1)}, u32[]{:S(2)}, u32[]{:S(2)}) collective-permute-start(f32[288,128]{1,0:T(8,128)S(1)} %get-tuple-element.12.flux), channel_id=1, source_target_pairs={{0,16},{16,0},{1,17},{17,1},{2,18},{18,2},{3,19},{19,3},{4,20},{20... | collective-permute-start | bytes 442376 | tf_op jit(solution)/shard_map/ppermute | solution.py:536
  115.0 1.4 %collective-permute-start.3 = (f32[288,128]{1,0:T(8,128)S(1)}, f32[288,128]{1,0:T(8,128)S(1)}, u32[]{:S(2)}, u32[]{:S(2)}) collective-permute-start(f32[288,128]{1,0:T(8,128)S(1)} %get-tuple-element.14), channel_id=1, source_target_pairs={{0,16},{16,0},{1,17},{17,1},{2,18},{18,2},{3,19},{19,3},{4,20},{20... | collective-permute-start | bytes 442376 | tf_op jit(solution)/shard_map/ppermute | solution.py:536
  116.6 2.8 %copy-start.3 = (f32[32,6,6144]{2,1,0:T(8,128)S(1)}, f32[32,6,6144]{2,1,0:T(8,128)}, u32[]{:S(2)}) copy-start(f32[32,6,6144]{2,1,0:T(8,128)} %copy-done.2) | copy-start | bytes 14155780
where the time goes:
time: 124 us
  Pallas kernels  102 us (82%)
  local copies, waits for them, and re-layouts  12.4 us (10%)
  waiting for transfers between devices  3.95 us (3%)
  starting transfers between devices  3.92 us (3%)
    pallas_call x2, Pallas kernels, exchange(): pl.pallas_call(functools.partial(exchange_kernel, tracers, sections, ring...  70.8 us
    pallas_call x1, Pallas kernels, setup(): pl.pallas_call(functools.partial(setup_kernel, devices, cap_rows), out_sh...  17.6 us
    unnamed x32, local copies, waits for them, and re-layouts  11.3 us
    pallas_call x1, Pallas kernels, descend(): pl.pallas_call(descend_kernel, grid=(columns // COL_TILE,), in_specs=[pl....  5.2 us
    pallas_call x1, Pallas kernels, ascend(): pl.pallas_call(ascend_kernel, grid=(columns // COL_TILE,), in_specs=[pl.B...  4.43 us
    pallas_call x1, Pallas kernels, descend_end(): pl.pallas_call(descend_end_kernel, grid=(columns // COL_TILE,), in_specs=...  4.15 us
    ppermute x1, starting transfers between devices, body(): handed = lax.ppermute(descend_end(air, mix_coef), 'sect', [(0, 1)])  2.5 us
  transfers between devices with their start and end apart: 4, of which 3 were waited for; matrix products, arithmetic and copies ran while one was open for 1% of the time, Pallas kernels for 14%

commit v1 on v0

v1 whole, which is shorter than its diff:
```python
import functools

import jax
import jax.numpy as jnp
from jax import lax
from jax.experimental import pallas as pl
from jax.experimental.pallas import tpu as pltpu
from jax.sharding import PartitionSpec as P

BLOCK_COLS = 128
BLOCK_SLOTS = 256
SUBSTEPS = 2
LANES = 128
COL_TILE = 1024
PARAMS = pltpu.CompilerParams(vmem_limit_bytes=40 * 1024 * 1024)


def split(value):
    high = value.astype(jnp.bfloat16).astype(jnp.float32)
    return high, value - high


def hot(index, count):
    places = lax.broadcasted_iota(jnp.int32, (count, index.shape[1]), 0).astype(jnp.int16)
    return jnp.where(places == index.astype(jnp.int16), jnp.ones((), jnp.bfloat16), jnp.zeros((), jnp.bfloat16))


def in_line(packed):
    return jnp.concatenate([packed[r : r + 1] for r in range(packed.shape[0])], axis=1)


def in_rows(line):
    return jnp.concatenate([line[:, r : r + LANES] for r in range(0, line.shape[1], LANES)], axis=0)


def scatter(values, row, lane, rows):
    mask = hot(row, rows)
    parts = [split(value) for value in values]
    lines = [in_line(p[0]) for p in parts] + [in_line(p[1]) for p in parts]
    return lax.dot_general(
        jnp.concatenate([mask * line.astype(jnp.bfloat16) for line in lines], axis=0),
        hot(lane, LANES),
        (((1,), (1,)), ((), ())),
        preferred_element_type=jnp.float32,
    )


def table_of(value):
    high, low = split(value)
    return jnp.concatenate([high, low], axis=1).astype(jnp.bfloat16)


def gather(table, row, lane, rows):
    lane_hot = hot(lane, LANES)
    picked = jnp.dot(table, jnp.concatenate([lane_hot, lane_hot], axis=0), preferred_element_type=jnp.float32)
    mask = lax.broadcasted_iota(jnp.int32, (rows, row.shape[1]), 0) == row
    return [
        jnp.sum(jnp.where(mask, picked[q : q + rows], 0.0), axis=0, keepdims=True)
        for q in range(0, table.shape[0], rows)
    ]


def setup_kernel(devices, cap_rows, step, owner, column, coef, weight, counts, out, acc, offset):
    ring = devices // 2
    slots = step * LANES
    blocks = slots // BLOCK_SLOTS
    acc[...] = jnp.zeros_like(acc)
    offset[...] = jnp.zeros_like(offset)
    later = (
        lax.broadcasted_iota(jnp.int32, (BLOCK_SLOTS, BLOCK_SLOTS), 0)
        <= lax.broadcasted_iota(jnp.int32, (BLOCK_SLOTS, BLOCK_SLOTS), 1)
    )
    later = jnp.where(later, 1.0, 0.0).astype(jnp.bfloat16)
    places = devices * cap_rows
    numbers = lax.broadcasted_iota(jnp.int32, (step, LANES), 0)
    within = lax.rem(numbers, 2) * LANES + lax.broadcasted_iota(jnp.int32, (step, LANES), 1)

    def part(i, _):
        here = pl.ds(pl.multiple_of(i * step, step), step)
        own_packed = owner[here, :]
        own = in_line(own_packed)
        named = hot(own, devices)
        named_blocks = [named[:, b * BLOCK_SLOTS : (b + 1) * BLOCK_SLOTS] for b in range(blocks)]
        running = jnp.dot(jnp.concatenate(named_blocks, axis=0), later, preferred_element_type=jnp.float32)
        before = offset[...]
        ranks = []
        for b in range(blocks):
            wide = named_blocks[b].astype(jnp.float32)
            count = running[b * devices : (b + 1) * devices] + before[:, 0:1]
            ranks.append(jnp.sum(wide * count, axis=0, keepdims=True) - 1.0)
            before = before + jnp.broadcast_to(jnp.sum(wide, axis=1, keepdims=True), before.shape)
        offset[...] = before
        rank = jnp.concatenate(ranks, axis=1).astype(jnp.int32)
        gain = jnp.where(within < counts[here, :], coef[here, :], 0.0)
        flow = weight[here, :] * gain
        gain_high, gain_low = split(gain)
        flow_high, flow_low = split(flow)
        values = [
            ((i * step + numbers) // 2).astype(jnp.float32),
            column[here, :].astype(jnp.float32),
            gain_high,
            gain_low,
            flow_high,
            flow_low,
        ]
        row = (lax.rem(own, ring) * 2 + own // ring) * cap_rows + rank // LANES
        mask = hot(row, places)
        acc[...] += lax.dot_general(
            jnp.concatenate([mask * in_line(value).astype(jnp.bfloat16) for value in values], axis=0),
            hot(lax.rem(rank, LANES), LANES),
            (((1,), (1,)), ((), ())),
            preferred_element_type=jnp.float32,
        )
        return 0

    lax.fori_loop(0, owner.shape[0] // step, part, 0)
    out[0] = acc[0:places]
    out[1] = acc[places : 2 * places]
    out[2] = acc[2 * places : 3 * places] + acc[3 * places : 4 * places]
    out[3] = acc[4 * places : 5 * places] + acc[5 * places : 6 * places]


def setup(owner, column, coef, weight, counts, devices, cap_rows):
    places = devices * cap_rows
    step = max(2, min(16, 2048 // places))
    while owner.shape[0] % step:
        step -= 2
    return pl.pallas_call(
        functools.partial(setup_kernel, devices, cap_rows, step),
        out_shape=jax.ShapeDtypeStruct((4, places, LANES), jnp.float32),
        scratch_shapes=[
            pltpu.VMEM((6 * places, LANES), jnp.float32),
            pltpu.VMEM((devices, LANES), jnp.float32),
        ],
        compiler_params=PARAMS,
    )(owner, column, coef, weight, counts)


def level_down(mix, air, k, under, carried):
    coupling = mix[k : k + 1, :]
    inverse = 1.0 / (1.0 + coupling + under)
    part = (air[k] + carried) * inverse
    ratio = coupling * inverse
    return part, ratio, inverse, ratio * (1.0 + under), coupling * part


def descend_end_kernel(air, mix, end):
    under = jnp.zeros((1, end.shape[1]), jnp.float32)
    carried = jnp.zeros((air.shape[0], end.shape[1]), jnp.float32)
    levels_first = jnp.swapaxes(air[...], 0, 1)
    for k in range(air.shape[1]):
        _, _, _, under, carried = level_down(mix, levels_first, k, under, carried)
    end[...] = jnp.concatenate([carried, under], axis=0)


def descend_end(air, mix):
    tracers, levels, columns = air.shape
    return pl.pallas_call(
        descend_end_kernel,
        grid=(columns // COL_TILE,),
        in_specs=[
            pl.BlockSpec((tracers, levels, COL_TILE), lambda j: (0, 0, j)),
            pl.BlockSpec((levels, COL_TILE), lambda j: (0, j)),
        ],
        out_specs=pl.BlockSpec((tracers + 1, COL_TILE), lambda j: (0, j)),
        out_shape=jax.ShapeDtypeStruct((tracers + 1, columns), jnp.float32),
        compiler_params=PARAMS,
    )(air, mix)


def descend_kernel(air, mix, start, last, parts, ratios, ends):
    tracers, levels, _ = air.shape
    levels_first = jnp.swapaxes(air[...], 0, 1)
    carried = start[0:tracers, :]
    under = start[tracers : tracers + 1, :]
    for k in range(levels):
        part, ratio, inverse, under, carried = level_down(mix, levels_first, k, under, carried)
        parts[k] = part
        if k == levels - 1:
            ratio = last[...] * inverse
        ratios[k : k + 1, :] = ratio
    value, factor = part, ratio
    ends[0, 0:tracers, :] = part
    ends[0, tracers : tracers + 1, :] = ratio
    for k in range(levels - 2, -1, -1):
        ratio = ratios[k : k + 1, :]
        value = parts[k] + ratio * value
        factor = ratio * factor
    ends[1, 0:tracers, :] = value
    ends[1, tracers : tracers + 1, :] = factor


def descend(air, mix, start, last):
    tracers, levels, columns = air.shape
    return pl.pallas_call(
        descend_kernel,
        grid=(columns // COL_TILE,),
        in_specs=[
            pl.BlockSpec((tracers, levels, COL_TILE), lambda j: (0, 0, j)),
            pl.BlockSpec((levels, COL_TILE), lambda j: (0, j)),
            pl.BlockSpec((tracers + 1, COL_TILE), lambda j: (0, j)),
            pl.BlockSpec((1, COL_TILE), lambda j: (0, j)),
        ],
        out_specs=[
            pl.BlockSpec((levels, tracers, COL_TILE), lambda j: (0, 0, j)),
            pl.BlockSpec((levels, COL_TILE), lambda j: (0, j)),
            pl.BlockSpec((2, tracers + 1, COL_TILE), lambda j: (0, 0, j)),
        ],
        out_shape=[
            jax.ShapeDtypeStruct((levels, tracers, columns), jnp.float32),
            jax.ShapeDtypeStruct(mix.shape, jnp.float32),
            jax.ShapeDtypeStruct((2, tracers + 1, columns), jnp.float32),
        ],
        compiler_params=PARAMS,
    )(air, mix, start, last)


def ascend_kernel(parts, ratios, below, out):
    value = below[...]
    risen = []
    for k in range(parts.shape[0] - 1, -1, -1):
        value = parts[k] + ratios[k : k + 1, :] * value
        risen.append(value)
    out[...] = jnp.swapaxes(jnp.stack(risen[::-1]), 0, 1)


def ascend(parts, ratios, below):
    levels, tracers, columns = parts.shape
    return pl.pallas_call(
        ascend_kernel,
        grid=(columns // COL_TILE,),
        in_specs=[
            pl.BlockSpec((levels, tracers, COL_TILE), lambda j: (0, 0, j)),
            pl.BlockSpec((levels, COL_TILE), lambda j: (0, j)),
            pl.BlockSpec((tracers, COL_TILE), lambda j: (0, j)),
        ],
        out_specs=pl.BlockSpec((tracers, levels, COL_TILE), lambda j: (0, 0, j)),
        out_shape=jax.ShapeDtypeStruct((tracers, levels, columns), jnp.float32),
        compiler_params=PARAMS,
    )(parts, ratios, below)


def exchange_kernel(
    tracers,
    ring,
    cap_rows,
    resid,
    slope,
    sorted_cells,
    surface,
    sea,
    rate,
    flux_out,
    sea_out,
    cells,
    spots,
    waters,
    rates,
    col_row,
    col_lane,
    flow,
    gain_sent,
    gain_came,
    strength,
    inverse,
    flux,
    sent,
    arrived,
    back,
    returned,
    acc,
    total,
    send_sem,
    recv_sem,
    pair_send,
    pair_recv,
    local_sem,
):
    rows, surf_rows = slope.shape[0], rate.shape[0]
    mine = tracers // 2
    half = 2 * cap_rows
    whole = 2 * half
    sect = lax.axis_index("sect")
    me = lax.axis_index("cols")
    other = 1 - sect

    def ahead(s):
        return lax.rem(me + s, ring)

    def behind(s):
        return lax.rem(me + ring - s, ring)

    def to(phase, source, target, s):
        return pltpu.make_async_remote_copy(
            src_ref=source.at[ahead(s)],
            dst_ref=target.at[me],
            send_sem=send_sem.at[phase, s],
            recv_sem=recv_sem.at[phase, s],
            device_id=(sect, ahead(s)),
            device_id_type=pl.DeviceIdType.MESH,
        )

    def to_partner(k, source, target):
        return pltpu.make_async_remote_copy(
            src_ref=source,
            dst_ref=target,
            send_sem=pair_send.at[k],
            recv_sem=pair_recv.at[k],
            device_id=(other, me),
            device_id_type=pl.DeviceIdType.MESH,
        )

    def in_pairs(act):
        def far(i, _):
            act(ring // 2 + 2 * i, ring // 2 + 2 * i + 1)
            return 0

        def near(i, _):
            act(ring // 2 - 1 - 2 * i, ring // 2 - 2 - 2 * i)
            return 0

        lax.fori_loop(0, ring // 4, far, 0)
        lax.fori_loop(0, ring // 4 - 1, near, 0)
        act(1, 0)

    barrier = pltpu.get_barrier_semaphore()

    def greet(s, _):
        pl.semaphore_signal(barrier, inc=1, device_id=(sect, ahead(s)), device_id_type=pl.DeviceIdType.MESH)
        return 0

    lax.fori_loop(1, ring, greet, 0)
    pl.semaphore_signal(barrier, inc=1, device_id=(other, me), device_id_type=pl.DeviceIdType.MESH)
    pl.semaphore_wait(barrier, ring)

    their_sea = sea.at[pl.ds(pl.multiple_of(other * (mine * surf_rows), 8), mine * surf_rows)]
    my_sea = sea.at[pl.ds(pl.multiple_of(sect * (mine * surf_rows), 8), mine * surf_rows)]
    shared = [
        to_partner(0, sorted_cells, cells.at[sect]),
        to_partner(1, surface, spots.at[sect]),
        to_partner(2, their_sea, waters.at[sect]),
        to_partner(3, rate, rates.at[sect]),
    ]
    kept = [
        pltpu.make_async_copy(sorted_cells, cells.at[sect], local_sem.at[0]),
        pltpu.make_async_copy(surface, spots.at[sect], local_sem.at[1]),
        pltpu.make_async_copy(my_sea, waters.at[sect], local_sem.at[2]),
        pltpu.make_async_copy(rate, rates.at[sect], local_sem.at[3]),
    ]
    for copy in shared + kept:
        copy.start()
    flux[...] = jnp.zeros_like(flux)
    for copy in kept:
        copy.wait()
    for copy in shared:
        copy.wait()

    def arrange(chip, _):
        here = pl.ds(pl.multiple_of(chip * half, 8), half)

        def merged(v):
            upper, lower = cells[0, v, here, :], cells[1, v, here, :]
            return jnp.concatenate(
                [upper[0:cap_rows], lower[0:cap_rows], upper[cap_rows:], lower[cap_rows:]], axis=0
            )

        col_row[chip] = merged(0).astype(jnp.int32)
        col_lane[chip] = merged(1).astype(jnp.int32)
        gain_sent[chip] = merged(2)
        flow[chip] = merged(3)
        return 0

    lax.fori_loop(0, ring, arrange, 0)

    def send_gain(s, _):
        to(0, gain_sent, gain_came, s).start()
        return 0

    lax.fori_loop(1, ring, send_gain, 0)
    gain_came[me] = gain_sent[me]
    my_resid = resid.at[pl.ds(pl.multiple_of(sect * (mine * rows), 8), mine * rows)]

    def spot(v, d, chips):
        return in_line(
            jnp.concatenate(
                [spots[d, v, pl.ds(pl.multiple_of(chip * half, 8), half), :] for chip in chips], axis=0
            )
        ).astype(jnp.int32)

    for step in range(SUBSTEPS):
        out_phase, back_phase = 1 + 2 * step, 2 + 2 * step
        bottom = my_resid[...] + jnp.concatenate([slope[...]] * mine, axis=0) * flux[...]
        table = table_of(bottom)

        def send(*steps):
            chips = [ahead(s) for s in steps]
            row = in_line(jnp.concatenate([col_row[chip] for chip in chips], axis=0))
            lane = in_line(jnp.concatenate([col_lane[chip] for chip in chips], axis=0))
            picked = [in_rows(p) for p in gather(table, row, lane, rows)]
            for j, (s, chip) in enumerate(zip(steps, chips)):
                for q in range(mine):
                    sent[chip, q * whole : (q + 1) * whole, :] = picked[q][j * whole : (j + 1) * whole]
                if not (isinstance(s, int) and s == 0):
                    to(out_phase, sent, arrived, s).start()

        in_pairs(send)
        arrived[me] = sent[me]
        acc[...] = jnp.zeros_like(acc)
        if step == 0:
            total[...] = jnp.zeros_like(total)

        def receive(*steps):
            chips = [behind(s) for s in steps]
            for s in steps:
                if not (isinstance(s, int) and s == 0):
                    if step == 0:
                        to(0, gain_sent, gain_came, s).wait_recv()
                    to(out_phase, sent, arrived, s).wait_recv()
            for d in range(2):
                row, lane = spot(0, d, chips), spot(1, d, chips)
                force = []
                for chip in chips:
                    if step == 0:
                        frac = spots[d, 2, pl.ds(pl.multiple_of(chip * half, 8), half), :]
                        strength[chip, d * half : (d + 1) * half, :] = (
                            gain_came[chip, d * half : (d + 1) * half, :] * frac
                        )
                    force.append(strength[chip, d * half : (d + 1) * half, :])
                values = [
                    jnp.concatenate(
                        [
                            arrived[chip, q * whole + d * half : q * whole + (d + 1) * half, :] * f
                            for chip, f in zip(chips, force)
                        ],
                        axis=0,
                    )
                    for q in range(mine)
                ]
                if step == 0:
                    values.append(jnp.concatenate(force, axis=0))
                summed = scatter(values, row, lane, surf_rows)
                span = len(values) * surf_rows
                wide = mine * surf_rows
                acc[d] += summed[0:wide] + summed[span : span + wide]
                if step == 0:
                    total[d] += summed[wide:span] + summed[span + wide :]

        in_pairs(receive)
        for d in range(2):
            if step == 0:
                inverse[d] = 1.0 / (1.0 + rates[d] * total[d])
            for q in range(mine):
                here = slice(q * surf_rows, (q + 1) * surf_rows)
                waters[d, here, :] = (waters[d, here, :] + rates[d] * acc[d, here, :]) * inverse[d]
        tables = [table_of(waters[d]) for d in range(2)]
        if step == 1:
            pass

        def give_back(*steps):
            chips = [ahead(s) for s in steps]
            for d in range(2):
                picked = [in_rows(p) for p in gather(tables[d], spot(0, d, chips), spot(1, d, chips), surf_rows)]
                for j, chip in enumerate(chips):
                    for q in range(mine):
                        back[chip, q * whole + d * half : q * whole + (d + 1) * half, :] = picked[q][
                            j * half : (j + 1) * half
                        ]
            for s in steps:
                if not (isinstance(s, int) and s == 0):
                    to(back_phase, back, returned, s).start()

        in_pairs(give_back)
        returned[me] = back[me]
        flux[...] = jnp.zeros_like(flux)

        def take_back(*steps):
            chips = [behind(s) for s in steps]
            for s in steps:
                if not (isinstance(s, int) and s == 0):
                    to(back_phase, back, returned, s).wait_recv()
            values = []
            for q in range(mine):
                here = slice(q * whole, (q + 1) * whole)
                values.append(
                    jnp.concatenate(
                        [(returned[chip, here, :] - sent[chip, here, :]) * flow[chip] for chip in chips], axis=0
                    )
                )
            row = in_line(jnp.concatenate([col_row[chip] for chip in chips], axis=0))
            lane = in_line(jnp.concatenate([col_lane[chip] for chip in chips], axis=0))
            summed = scatter(values, row, lane, rows)
            flux[...] += summed[0 : mine * rows] + summed[mine * rows :]

        in_pairs(take_back)

        def finish(s, _):
            if step == 0:
                to(0, gain_sent, gain_came, s).wait_send()
            to(out_phase, sent, arrived, s).wait_send()
            to(back_phase, back, returned, s).wait_send()
            return 0

        lax.fori_loop(1, ring, finish, 0)

    flux_here = flux_out.at[pl.ds(pl.multiple_of(sect * (mine * rows), 8), mine * rows)]
    sea_here = sea_out.at[pl.ds(pl.multiple_of(sect * (mine * surf_rows), 8), mine * surf_rows)]
    last = [
        to_partner(4, flux, flux_here),
        to_partner(5, waters.at[other], sea_here),
    ]
    stay = [
        pltpu.make_async_copy(flux, flux_here, local_sem.at[4]),
        pltpu.make_async_copy(waters.at[sect], sea_here, local_sem.at[5]),
    ]
    for copy in last + stay:
        copy.start()
    for copy in last + stay:
        copy.wait()


def exchange(tracers, ring, cap_rows, resid, slope, sorted_cells, surface, sea, rate):
    rows, surf_rows = slope.shape[0], rate.shape[0]
    mine = tracers // 2
    whole = 4 * cap_rows
    real = lambda *shape: pltpu.VMEM(shape, jnp.float32)
    message = real(ring, mine * whole, LANES)
    once = real(ring, whole, LANES)
    return pl.pallas_call(
        functools.partial(exchange_kernel, tracers, ring, cap_rows),
        out_shape=[
            jax.ShapeDtypeStruct(resid.shape, jnp.float32),
            jax.ShapeDtypeStruct(sea.shape, jnp.float32),
        ],
        in_specs=[pl.BlockSpec(memory_space=pltpu.VMEM)] * 6,
        out_specs=[pl.BlockSpec(memory_space=pltpu.VMEM)] * 2,
        scratch_shapes=[
            real(2, *sorted_cells.shape),
            real(2, *surface.shape),
            real(2, mine * surf_rows, LANES),
            real(2, surf_rows, LANES),
            pltpu.VMEM((ring, whole, LANES), jnp.int32),
            pltpu.VMEM((ring, whole, LANES), jnp.int32),
            once,
            once,
            once,
            once,
            real(2, surf_rows, LANES),
            real(mine * rows, LANES),
            message,
            message,
            message,
            message,
            real(2, mine * surf_rows, LANES),
            real(2, surf_rows, LANES),
            pltpu.SemaphoreType.DMA((1 + 2 * SUBSTEPS, ring)),
            pltpu.SemaphoreType.DMA((1 + 2 * SUBSTEPS, ring)),
            pltpu.SemaphoreType.DMA((6,)),
            pltpu.SemaphoreType.DMA((6,)),
            pltpu.SemaphoreType.DMA((6,)),
        ],
        compiler_params=pltpu.CompilerParams(
            vmem_limit_bytes=40 * 1024 * 1024, collective_id=0, has_side_effects=True
        ),
    )(resid, slope, sorted_cells, surface, sea, rate)


def body(
    air_state,
    mix_coef,
    flux_scale,
    sea_state,
    sea_rate,
    block_counts,
    cell_column,
    cell_owner,
    cell_coef,
    cell_weight,
    slot_cell,
    slot_frac,
):
    levels, tracers, columns = air_state.shape
    is_lower = lax.axis_index("sect") == 1
    ring = lax.axis_size("cols")
    devices = 2 * ring
    rows = columns // BLOCK_COLS
    surf_cells = sea_state.shape[1]
    surf_rows = surf_cells // LANES
    capacity = slot_cell.shape[0] // devices
    cap_rows = max(4, -(-capacity // LANES))

    air = jnp.swapaxes(air_state, 0, 1)
    handed = lax.ppermute(descend_end(air, mix_coef), "sect", [(0, 1)])
    sorted_cells = setup(
        cell_owner.reshape(-1, LANES),
        cell_column.reshape(-1, LANES),
        cell_coef.reshape(-1, LANES),
        cell_weight.reshape(-1, LANES),
        jnp.broadcast_to(block_counts.reshape(-1, 1, 1), (rows, 2, LANES)).reshape(-1, LANES),
        devices,
        cap_rows,
    )

    def by_chip(values):
        values = jnp.pad(values.reshape(2, ring, capacity), ((0, 0), (0, 0), (0, cap_rows * LANES - capacity)))
        values = jnp.swapaxes(values.reshape(2, ring, cap_rows, LANES), 0, 1)
        return values.reshape(ring * 2 * cap_rows, LANES)

    cell = by_chip(slot_cell)
    surface = jnp.stack(
        [(cell // LANES).astype(jnp.float32), (cell % LANES).astype(jnp.float32), by_chip(slot_frac)]
    )

    last = jnp.where(is_lower, flux_scale, mix_coef[-1])[None]
    parts, ratios, ends = descend(air, mix_coef, handed, last)
    received = lax.ppermute(ends, "sect", [(1, 0)])
    low = jnp.where(is_lower, ends, received)
    resid = low[0, :tracers].reshape(tracers * rows, LANES)
    slope = low[0, tracers].reshape(rows, LANES)

    flux, sea = exchange(
        tracers,
        ring,
        cap_rows,
        resid,
        slope,
        sorted_cells,
        surface,
        sea_state.reshape(tracers * surf_rows, LANES),
        sea_rate.reshape(surf_rows, LANES),
    )
    flux_col = flux.reshape(tracers, columns)
    below = jnp.where(is_lower, flux_col, low[1, :tracers] + low[1, tracers] * flux_col)
    return (jnp.swapaxes(ascend(parts, ratios, below), 0, 1), sea.reshape(tracers, surf_cells))


def solution(mesh):
    return jax.shard_map(
        body,
        mesh=mesh,
        in_specs=(
            P("sect", None, "cols"),
            P("sect", "cols"),
            P("cols"),
            P(None, ("sect", "cols")),
            P(("sect", "cols")),
            P(("sect", "cols"), None),
            P(("sect", "cols")),
            P(("sect", "cols"), None),
            P(("sect", "cols")),
            P(("sect", "cols")),
            P(("sect", "cols")),
            P(("sect", "cols")),
        ),
        out_specs=(P("sect", None, "cols"), P(None, ("sect", "cols"))),
        check_vma=False,
    )
```

time: 124 us -> 107 us (0.86)
  Pallas kernels: 102 us -> 87.2 us
  waiting for transfers between devices: 3.95 us -> 2.04 us
    pallas_call x3 -> x2, Pallas kernels: 88.5 us -> 73.4 us  [the longest x1 66.2 us: exchange(): pl.pallas_call(functools.partial(exchange_kernel, tracers, ring, cap_rows...]
    ppermute x2 -> x0, waiting for transfers between devices: 2.06 us -> none  [body(): other = lax.ppermute(flux, 'sect', [(0, 1), (1, 0)])]
  transfers between devices with their start and end apart: 4 -> 2, of which waited for: 3 -> 1; matrix products, arithmetic and copies ran while one was open for 1% -> 1% of each run, Pallas kernels for 14% -> 7%
where the time goes in v1:
time: 107 us
  Pallas kernels  87.2 us (81%)
  local copies, waits for them, and re-layouts  12.7 us (12%)
  starting transfers between devices  3.83 us (4%)
  waiting for transfers between devices  2.04 us (2%)
    pallas_call x1, Pallas kernels, exchange(): pl.pallas_call(functools.partial(exchange_kernel, tracers, ring, cap_rows...  66.2 us
    unnamed x32, local copies, waits for them, and re-layouts  11.3 us
    pallas_call x1, Pallas kernels, setup(): pl.pallas_call(functools.partial(setup_kernel, devices, cap_rows, step),...  7.21 us
    pallas_call x1, Pallas kernels, descend(): pl.pallas_call(descend_kernel, grid=(columns // COL_TILE,), in_specs=[pl....  5.2 us
    pallas_call x1, Pallas kernels, ascend(): pl.pallas_call(ascend_kernel, grid=(columns // COL_TILE,), in_specs=[pl.B...  4.43 us
    pallas_call x1, Pallas kernels, descend_end(): pl.pallas_call(descend_end_kernel, grid=(columns // COL_TILE,), in_specs=...  4.15 us
    ppermute x1, starting transfers between devices, body(): handed = lax.ppermute(descend_end(air, mix_coef), 'sect', [(0, 1)])  2.37 us
  transfers between devices with their start and end apart: 2, of which 1 were waited for; matrix products, arithmetic and copies ran while one was open for 1% of the time, Pallas kernels for 7%

profile of v1, /device:TPU:0, one launch (start us, length us, event | category | flops | bytes accessed | tf_op | source)
XLA Modules:
  0.0 106.9 jit_solution(18261938345660356915)
XLA Ops:
  0.6 0.0 copy-start
  0.7 2.3 %copy-done = f32[32,6,6144]{2,0,1:T(8,128)S(1)} copy-done((f32[32,6,6144]{2,0,1:T(8,128)S(1)}, f32[32,6,6144]{2,0,1:T(8,128)}, u32[]{:S(2)}) %copy-start) | copy-done | bytes 4718616
  3.0 1.1 %copy-done.4 = f32[32,6144]{1,0:T(8,128)S(1)} copy-done((f32[32,6144]{1,0:T(8,128)S(1)}, f32[32,6144]{1,0:T(8,128)}, u32[]{:S(2)}) %copy-start.4) | copy-done | bytes 786456
  4.2 4.2 %shard_map.131 = f32[7,6144]{1,0:T(8,128)S(1)} custom-call(f32[6,32,6144]{2,1,0:T(8,128)S(1)} %bitcast.24, f32[32,6144]{1,0:T(8,128)S(1)} %copy-done.4), custom_call_target="tpu_custom_call" | custom-call | tf_op jit(solution)/shard_map/pallas_call | solution.py:158
  8.3 2.4 %collective-permute-start = (f32[7,6144]{1,0:T(8,128)S(1)}, f32[7,6144]{1,0:T(8,128)S(1)}, u32[]{:S(2)}, u32[]{:S(2)}) collective-permute-start(f32[7,6144]{1,0:T(8,128)S(1)} %shard_map.131), channel_id=1, source_target_pairs={{0,16},{1,17},{2,18},{3,19},{4,20},{5,21},{6,22},{7,23},{8,24},{9,... | collective-permute-start | bytes 516104 | tf_op jit(solution)/shard_map/ppermute | solution.py:592
  10.8 0.1 broadcast_in_dim.16
  10.8 0.1 broadcast_in_dim.17
  11.0 0.1 reshape.160
  11.2 0.1 reshape.163
  11.3 0.0 copy-start.10
  11.4 0.1 broadcast_in_dim.18.counts
  11.5 7.2 %shard_map.133.sorted_cells = f32[4,128,128]{2,1,0:T(8,128)S(1)} custom-call(s32[96,128]{1,0:T(8,128)S(1)} %bitcast.28, s32[96,128]{1,0:T(8,128)S(1)} %bitcast.29, f32[96,128]{1,0:T(8,128)S(1)} %bitcast.30, f32[96,128]{1,0:T(8,128)S(1)} %bitcast.31, s32[96,128]{1,0:T(8,128)S(1)} %broadcast_in_dim.18.counts), custom_call_target="tpu_custom_call" | custom-call | tf_op jit(solution)/shard_map/pallas_call | solution.py:128
  18.7 2.3 %copy-done.1 = f32[32,6,6144]{2,0,1:T(8,128)S(1)} copy-done((f32[32,6,6144]{2,0,1:T(8,128)S(1)}, f32[32,6,6144]{2,0,1:T(8,128)}, u32[]{:S(2)}) %copy-start.1) | copy-done | bytes 4718616
  21.1 5.2 %shard_map.132 = (f32[32,6,6144]{2,1,0:T(8,128)S(1)}, f32[32,6144]{1,0:T(8,128)S(1)}, f32[2,7,6144]{2,1,0:T(8,128)S(1)}) custom-call(f32[6,32,6144]{2,1,0:T(8,128)S(1)} %bitcast.25, f32[32,6144]{1,0:T(8,128)S(1)} %copy-done.5, f32[7,6144]{1,0:T(8,128)S(1)} %collective-permute-done.start, f32[1,6144]{1,0:T(1,128)S(1)} %bitcast.26), custom_call_target="tpu_custom_call" | custom-call | tf_op jit(solution)/shard_map/pallas_call | solution.py:195
  26.3 2.7 %copy-done.2 = f32[32,6,6144]{2,1,0:T(8,128)} copy-done((f32[32,6,6144]{2,1,0:T(8,128)}, f32[32,6,6144]{2,1,0:T(8,128)S(1)}, u32[]{:S(2)}) %copy-start.2) | copy-done | bytes 4718616
  28.9 1.5 %collective-permute-start.1 = (f32[2,7,6144]{2,1,0:T(8,128)S(1)}, f32[2,7,6144]{2,1,0:T(8,128)S(1)}, u32[]{:S(2)}, u32[]{:S(2)}) collective-permute-start(f32[2,7,6144]{2,1,0:T(8,128)S(1)} %get-tuple-element.9), channel_id=1, source_target_pairs={{16,0},{17,1},{18,2},{19,3},{20,4},{21,5},{22,6},{23,7},{24,8},{25... | collective-permute-start | bytes 1032200 | tf_op jit(solution)/shard_map/ppermute | solution.py:615
  30.4 0.1 fusion.2
  30.5 2.0 %collective-permute-done.1 = f32[2,7,6144]{2,1,0:T(8,128)S(1)} collective-permute-done((f32[2,7,6144]{2,1,0:T(8,128)S(1)}, f32[2,7,6144]{2,1,0:T(8,128)S(1)}, u32[]{:S(2)}, u32[]{:S(2)}) %collective-permute-start.1) | collective-permute-done | bytes 344096 | tf_op jit(solution)/shard_map/ppermute | solution.py:615
  32.5 0.1 broadcast_select_fusion
  32.6 0.1 fusion.6
  32.8 66.2 %shard_map.134 = (f32[288,128]{1,0:T(8,128)S(1)}, f32[144,128]{1,0:T(8,128)S(1)}) custom-call(f32[288,128]{1,0:T(8,128)S(1)} %reshape_squeeze.6.resid, f32[48,128]{1,0:T(8,128)S(1)} %bitcast.27, f32[4,128,128]{2,1,0:T(8,128)S(1)} %shard_map.133.sorted_cells, f32[3,128,128]{2,1,0:T(8,128)S(1)} %pad_maximum_fusion.surface, f32[144,128]{1,0:T(8,128)S(1)} %reshape.165.sea, ...), custom_call_target="tpu_custom_call" | custom-call | tf_op jit(solution)/shard_map/pallas_call | solution.py:528
  99.0 0.7 reshape.168
  99.7 2.8 %copy-done.3 = f32[32,6,6144]{2,1,0:T(8,128)S(1)} copy-done((f32[32,6,6144]{2,1,0:T(8,128)S(1)}, f32[32,6,6144]{2,1,0:T(8,128)}, u32[]{:S(2)}) %copy-start.3) | copy-done | bytes 4718616
  102.5 4.4 %shard_map.135 = f32[6,32,6144]{2,1,0:T(8,128)} custom-call(f32[32,6,6144]{2,1,0:T(8,128)S(1)} %copy-done.3, f32[32,6144]{1,0:T(8,128)S(1)} %get-tuple-element.8.ratios, f32[6,6144]{1,0:T(8,128)S(1)} %fusion.1.below), custom_call_target="tpu_custom_call" | custom-call | tf_op jit(solution)/shard_map/pallas_call | solution.py:229
  (40 shorter events, 0.3 us)
Async XLA Ops:
  0.6 10.1 %copy-start.15 = (s32[1,48]{1,0:T(1,128)S(1)}, s32[1,48]{1,0:T(1,128)}, u32[]{:S(2)}) copy-start(s32[1,48]{1,0:T(1,128)} %param.17) | copy-start | bytes 580
  0.6 2.3 %copy-start = (f32[32,6,6144]{2,0,1:T(8,128)S(1)}, f32[32,6,6144]{2,0,1:T(8,128)}, u32[]{:S(2)}) copy-start(f32[32,6,6144]{2,0,1:T(8,128)} %param.12) | copy-start | bytes 14155780
  3.0 1.1 %copy-start.4 = (f32[32,6144]{1,0:T(8,128)S(1)}, f32[32,6144]{1,0:T(8,128)}, u32[]{:S(2)}) copy-start(f32[32,6144]{1,0:T(8,128)} %mix.3) | copy-start | bytes 2359300
  4.1 6.8 %copy-start.12 = (s32[15360]{0:T(1024)S(1)}, s32[15360]{0:T(1024)}, u32[]{:S(2)}) copy-start(s32[15360]{0:T(1024)} %param.22) | copy-start | bytes 184324
  4.1 7.0 %copy-start.13 = (f32[15360]{0:T(1024)S(1)}, f32[15360]{0:T(1024)}, u32[]{:S(2)}) copy-start(f32[15360]{0:T(1024)} %param.23) | copy-start | bytes 184324
  4.1 7.2 %copy-start.11 = (f32[6,3072]{1,0:T(8,128)S(1)}, f32[6,3072]{1,0:T(8,128)}, u32[]{:S(2)}) copy-start(f32[6,3072]{1,0:T(8,128)} %param.15) | copy-start | bytes 221188
  4.1 7.3 %copy-start.6 = (s32[12288,1]{0,1:T(1,128)S(1)}, s32[12288,1]{0,1:T(1,128)}, u32[]{:S(2)}) copy-start(s32[12288,1]{0,1:T(1,128)} %param.19) | copy-start | bytes 147460
  4.1 7.3 %copy-start.7 = (s32[12288]{0:T(1024)S(1)}, s32[12288]{0:T(1024)}, u32[]{:S(2)}) copy-start(s32[12288]{0:T(1024)} %param.18) | copy-start | bytes 147460
  4.1 7.3 %copy-start.8 = (f32[12288]{0:T(1024)S(1)}, f32[12288]{0:T(1024)}, u32[]{:S(2)}) copy-start(f32[12288]{0:T(1024)} %param.20) | copy-start | bytes 147460
  4.2 7.3 %copy-start.9 = (f32[12288]{0:T(1024)S(1)}, f32[12288]{0:T(1024)}, u32[]{:S(2)}) copy-start(f32[12288]{0:T(1024)} %param.21) | copy-start | bytes 147460
  4.2 14.5 %copy-start.14 = (f32[6144]{0:T(1024)S(1)}, f32[6144]{0:T(1024)}, u32[]{:S(2)}) copy-start(f32[6144]{0:T(1024)} %param.14) | copy-start | bytes 73732
  4.2 14.5 %copy-start.5 = (f32[32,6144]{1,0:T(8,128)S(1)}, f32[32,6144]{1,0:T(8,128)}, u32[]{:S(2)}) copy-start(f32[32,6144]{1,0:T(8,128)} %mix.3) | copy-start | bytes 2359300
  8.3 10.4 %collective-permute-start = (f32[7,6144]{1,0:T(8,128)S(1)}, f32[7,6144]{1,0:T(8,128)S(1)}, u32[]{:S(2)}, u32[]{:S(2)}) collective-permute-start(f32[7,6144]{1,0:T(8,128)S(1)} %shard_map.131), channel_id=1, source_target_pairs={{0,16},{1,17},{2,18},{3,19},{4,20},{5,21},{6,22},{7,23},{8,24},{9,... | collective-permute-start | bytes 516104 | tf_op jit(solution)/shard_map/ppermute | solution.py:592
  11.3 21.5 %copy-start.10 = (f32[3072]{0:T(1024)S(1)}, f32[3072]{0:T(1024)}, u32[]{:S(2)}) copy-start(f32[3072]{0:T(1024)} %param.16) | copy-start | bytes 36868
  18.7 2.3 %copy-start.1 = (f32[32,6,6144]{2,0,1:T(8,128)S(1)}, f32[32,6,6144]{2,0,1:T(8,128)}, u32[]{:S(2)}) copy-start(f32[32,6,6144]{2,0,1:T(8,128)} %param.12) | copy-start | bytes 14155780
  26.3 2.7 %copy-start.2 = (f32[32,6,6144]{2,1,0:T(8,128)}, f32[32,6,6144]{2,1,0:T(8,128)S(1)}, u32[]{:S(2)}) copy-start(f32[32,6,6144]{2,1,0:T(8,128)S(1)} %get-tuple-element.7.parts) | copy-start | bytes 14155780
  28.9 3.6 %collective-permute-start.1 = (f32[2,7,6144]{2,1,0:T(8,128)S(1)}, f32[2,7,6144]{2,1,0:T(8,128)S(1)}, u32[]{:S(2)}, u32[]{:S(2)}) collective-permute-start(f32[2,7,6144]{2,1,0:T(8,128)S(1)} %get-tuple-element.9), channel_id=1, source_target_pairs={{16,0},{17,1},{18,2},{19,3},{20,4},{21,5},{22,6},{23,7},{24,8},{25... | collective-permute-start | bytes 1032200 | tf_op jit(solution)/shard_map/ppermute | solution.py:615
  99.7 2.8 %copy-start.3 = (f32[32,6,6144]{2,1,0:T(8,128)S(1)}, f32[32,6,6144]{2,1,0:T(8,128)}, u32[]{:S(2)}) copy-start(f32[32,6,6144]{2,1,0:T(8,128)} %copy-done.2) | copy-start | bytes 14155780

commit v2 on v1

v2 whole, which is shorter than its diff:
```python
import functools

import jax
import jax.numpy as jnp
from jax import lax
from jax.experimental import pallas as pl
from jax.experimental.pallas import tpu as pltpu
from jax.sharding import PartitionSpec as P

BLOCK_COLS = 128
BLOCK_SLOTS = 256
SUBSTEPS = 2
GROUPS = 2
LANES = 128
VMEM = pl.BlockSpec(memory_space=pltpu.VMEM)
HBM = pl.BlockSpec(memory_space=pltpu.HBM)


def split(value):
    high = value.astype(jnp.bfloat16).astype(jnp.float32)
    return high, value - high


def hot(index, count):
    places = lax.broadcasted_iota(jnp.int32, (count, index.shape[1]), 0).astype(jnp.int16)
    return jnp.where(places == index.astype(jnp.int16), jnp.ones((), jnp.bfloat16), jnp.zeros((), jnp.bfloat16))


def in_line(packed):
    return jnp.concatenate([packed[r : r + 1] for r in range(packed.shape[0])], axis=1)


def in_rows(line):
    return jnp.concatenate([line[:, r : r + LANES] for r in range(0, line.shape[1], LANES)], axis=0)


def scatter(values, row, lane, rows):
    mask = hot(row, rows)
    parts = [split(value) for value in values]
    lines = [in_line(p[0]) for p in parts] + [in_line(p[1]) for p in parts]
    return lax.dot_general(
        jnp.concatenate([mask * line.astype(jnp.bfloat16) for line in lines], axis=0),
        hot(lane, LANES),
        (((1,), (1,)), ((), ())),
        preferred_element_type=jnp.float32,
    )


def table_of(value):
    high, low = split(value)
    return jnp.concatenate([high, low], axis=1).astype(jnp.bfloat16)


def gather(table, row, lane, rows):
    lane_hot = hot(lane, LANES)
    picked = jnp.dot(table, jnp.concatenate([lane_hot, lane_hot], axis=0), preferred_element_type=jnp.float32)
    mask = lax.broadcasted_iota(jnp.int32, (rows, row.shape[1]), 0) == row
    return [
        jnp.sum(jnp.where(mask, picked[q : q + rows], 0.0), axis=0, keepdims=True)
        for q in range(0, table.shape[0], rows)
    ]


def forward_kernel(
    tracers,
    ring,
    cap_rows,
    step_rows,
    air,
    mix,
    scale,
    owner,
    column,
    coef,
    weight,
    counts,
    spots,
    sea,
    rate,
    parts,
    ratios,
    below,
    sea_out,
    mixes,
    inverses,
    hand,
    low,
    top,
    place_acc,
    offset,
    sorted_cells,
    cells,
    col_row,
    col_lane,
    flow,
    gain_sent,
    gain_came,
    strength,
    inverse,
    sent,
    arrived,
    back,
    returned,
    flux,
    flux_came,
    acc,
    send_sem,
    recv_sem,
    pair_send,
    pair_recv,
    local_sem,
    load_sem,
):
    levels, rows = ratios.shape[0], ratios.shape[1]
    surf_rows = rate.shape[0]
    devices = 2 * ring
    mine = tracers // GROUPS
    spot_rows = 2 * cap_rows
    sect = lax.axis_index("sect")
    me = lax.axis_index("cols")
    other = 1 - sect

    def ahead(s):
        return lax.rem(me + s, ring)

    def behind(s):
        return lax.rem(me + ring - s, ring)

    def remote(s):
        return not (isinstance(s, int) and s == 0)

    def to(phase, source, target, s):
        return pltpu.make_async_remote_copy(
            src_ref=source.at[ahead(s)],
            dst_ref=target.at[me],
            send_sem=send_sem.at[phase, s],
            recv_sem=recv_sem.at[phase, s],
            device_id=(sect, ahead(s)),
            device_id_type=pl.DeviceIdType.MESH,
        )

    def outward(step, g, s):
        return to(1 + 2 * (step * GROUPS + g), sent.at[g], arrived.at[g], s)

    def homeward(step, g, s):
        return to(2 + 2 * (step * GROUPS + g), back.at[g], returned.at[g], s)

    def to_partner(k, source, target):
        return pltpu.make_async_remote_copy(
            src_ref=source,
            dst_ref=target,
            send_sem=pair_send.at[k],
            recv_sem=pair_recv.at[k],
            device_id=(other, me),
            device_id_type=pl.DeviceIdType.MESH,
        )

    def flux_over(step, g):
        return to_partner(1 + step * GROUPS + g, flux.at[step, g], flux_came.at[step, g])

    def in_fours(act):
        def far(i, _):
            act(*[ring // 2 + 4 * i + j for j in range(4)])
            return 0

        def near(i, _):
            act(*[ring // 2 - 1 - 4 * i - j for j in range(4)])
            return 0

        lax.fori_loop(0, ring // 8, far, 0)
        lax.fori_loop(0, ring // 8 - 1, near, 0)
        act(3, 2, 1, 0)

    def line_of(ref, chips):
        return in_line(jnp.concatenate([ref[chip] for chip in chips], axis=0))

    def spot(v, chips):
        return in_line(
            jnp.concatenate(
                [spots[v, pl.ds(pl.multiple_of(chip * spot_rows, 8), spot_rows), :] for chip in chips], axis=0
            )
        ).astype(jnp.int32)

    barrier = pltpu.get_barrier_semaphore()

    def greet(s, _):
        pl.semaphore_signal(barrier, inc=1, device_id=(sect, ahead(s)), device_id_type=pl.DeviceIdType.MESH)
        return 0

    lax.fori_loop(1, ring, greet, 0)
    pl.semaphore_signal(barrier, inc=1, device_id=(other, me), device_id_type=pl.DeviceIdType.MESH)

    def load(j):
        here = pl.ds(pl.multiple_of(j * LANES, LANES), LANES)
        return [
            pltpu.make_async_copy(mix.at[:, here], mixes.at[:, j, :], load_sem.at[0, j]),
            pltpu.make_async_copy(air.at[:, :, here], parts.at[:, :, j, :], load_sem.at[1, j]),
        ]

    def start_load(j, _):
        for copy in load(j):
            copy.start()
        return 0

    def wait_load(j, _):
        for copy in load(j):
            copy.wait()
        return 0

    lax.fori_loop(0, rows, start_load, 0)

    places = devices * cap_rows
    blocks = step_rows * LANES // BLOCK_SLOTS
    place_acc[...] = jnp.zeros_like(place_acc)
    offset[...] = jnp.zeros_like(offset)
    later = (
        lax.broadcasted_iota(jnp.int32, (BLOCK_SLOTS, BLOCK_SLOTS), 0)
        <= lax.broadcasted_iota(jnp.int32, (BLOCK_SLOTS, BLOCK_SLOTS), 1)
    )
    later = jnp.where(later, 1.0, 0.0).astype(jnp.bfloat16)
    numbers = lax.broadcasted_iota(jnp.int32, (step_rows, LANES), 0)
    within = lax.rem(numbers, 2) * LANES + lax.broadcasted_iota(jnp.int32, (step_rows, LANES), 1)

    def sort_part(i, _):
        here = pl.ds(pl.multiple_of(i * step_rows, step_rows), step_rows)
        own = in_line(owner[here, :])
        named = hot(own, devices)
        named_blocks = [named[:, b * BLOCK_SLOTS : (b + 1) * BLOCK_SLOTS] for b in range(blocks)]
        running = jnp.dot(jnp.concatenate(named_blocks, axis=0), later, preferred_element_type=jnp.float32)
        before = offset[...]
        ranks = []
        for b in range(blocks):
            wide = named_blocks[b].astype(jnp.float32)
            count = running[b * devices : (b + 1) * devices] + before[:, 0:1]
            ranks.append(jnp.sum(wide * count, axis=0, keepdims=True) - 1.0)
            before = before + jnp.broadcast_to(jnp.sum(wide, axis=1, keepdims=True), before.shape)
        offset[...] = before
        rank = jnp.concatenate(ranks, axis=1).astype(jnp.int32)
        gain = jnp.where(within < counts[here, :], coef[here, :], 0.0)
        gain_high, gain_low = split(gain)
        flow_high, flow_low = split(weight[here, :] * gain)
        values = [
            ((i * step_rows + numbers) // 2).astype(jnp.float32),
            column[here, :].astype(jnp.float32),
            gain_high,
            gain_low,
            flow_high,
            flow_low,
        ]
        mask = hot(own * cap_rows + rank // LANES, places)
        place_acc[...] += lax.dot_general(
            jnp.concatenate([mask * in_line(value).astype(jnp.bfloat16) for value in values], axis=0),
            hot(lax.rem(rank, LANES), LANES),
            (((1,), (1,)), ((), ())),
            preferred_element_type=jnp.float32,
        )
        return 0

    def eliminate(under):
        def coefficients(k, under):
            coupling = mixes[k]
            inv = 1.0 / (1.0 + coupling + under)
            ratio = coupling * inv
            inverses[k] = inv
            ratios[k] = ratio
            return ratio * (1.0 + under)

        return lax.fori_loop(0, levels, coefficients, under, unroll=4)

    def descend(carried_of, keep):
        for q in range(0, tracers, 2):

            def level(k, carried):
                ratio, inv = ratios[k], inverses[k]
                result = []
                for j, value in enumerate(carried):
                    value = parts[q + j, k] + value
                    parts[q + j, k] = value * inv
                    result.append(value * ratio)
                return result

            keep(q, lax.fori_loop(0, levels, level, [carried_of(q), carried_of(q + 1)], unroll=4))

    handed = to_partner(1 + SUBSTEPS * GROUPS, hand, hand)
    lowest = to_partner(2 + SUBSTEPS * GROUPS, low, low)
    highest = to_partner(3 + SUBSTEPS * GROUPS, top, top)
    upper, lower = sect == 0, sect == 1

    def piece(q):
        return slice(q * rows, (q + 1) * rows)

    sort_steps = owner.shape[0] // step_rows
    early = sort_steps // 3
    lax.fori_loop(0, early, sort_part, 0)
    pl.semaphore_wait(barrier, ring)
    lax.fori_loop(0, rows, wait_load, 0)

    @pl.when(upper)
    def _():
        zero = jnp.zeros((rows, LANES), jnp.float32)
        hand[piece(tracers), :] = eliminate(zero)

        def keep(q, carried):
            hand[piece(q), :] = carried[0]
            hand[piece(q + 1), :] = carried[1]

        descend(lambda q: zero, keep)
        handed.start()

    lax.fori_loop(early, sort_steps, sort_part, 0)
    for v in range(2):
        sorted_cells[v] = place_acc[v * places : (v + 1) * places]
        first = (2 + 2 * v) * places
        sorted_cells[2 + v] = place_acc[first : first + places] + place_acc[first + places : first + 2 * places]

    def half_of(section):
        count = ring * cap_rows
        return sorted_cells.at[:, pl.ds(pl.multiple_of(section * count, 8), count), :]

    shared = to_partner(0, half_of(other), cells.at[sect])
    kept = pltpu.make_async_copy(half_of(sect), cells.at[sect], local_sem)
    shared.start()
    kept.start()

    @pl.when(lower)
    def _():
        handed.wait_recv()
        eliminate(hand[piece(tracers), :])
        ratios[levels - 1] = scale[...] * inverses[levels - 1]
        descend(lambda q: hand[piece(q), :], lambda q, carried: None)
        for q in range(tracers):
            low[piece(q), :] = parts[q, levels - 1]
        low[piece(tracers), :] = ratios[levels - 1]
        lowest.start()

    kept.wait()
    shared.wait()

    def arrange(i, _):
        here = pl.ds(pl.multiple_of(i * spot_rows, 8), spot_rows)

        def merged(v, k):
            piece = slice(k * cap_rows, (k + 1) * cap_rows)
            return jnp.concatenate([cells[0, v, here, :][piece], cells[1, v, here, :][piece]], axis=0)

        for k in range(2):
            col_row[2 * i + k] = merged(0, k).astype(jnp.int32)
            col_lane[2 * i + k] = merged(1, k).astype(jnp.int32)
            gain_sent[2 * i + k] = merged(2, k)
            flow[2 * i + k] = merged(3, k)
        return 0

    lax.fori_loop(0, ring // 2, arrange, 0)

    def send_gain(s, _):
        to(0, gain_sent, gain_came, s).start()
        return 0

    lax.fori_loop(1, ring, send_gain, 0)
    gain_came[me] = gain_sent[me]

    def send_all(step, g):
        here = slice(g * mine * rows, (g + 1) * mine * rows)
        bottom = low[here, :]
        if step:
            flux_over(step - 1, g).wait_recv()
            change = flux[step - 1, g] + flux_came[step - 1, g]
            bottom = bottom + jnp.concatenate([low[piece(tracers), :]] * mine, axis=0) * change
        table = table_of(bottom)

        def send(*steps):
            chips = [ahead(s) for s in steps]
            picked = [in_rows(p) for p in gather(table, line_of(col_row, chips), line_of(col_lane, chips), rows)]
            for j, (s, chip) in enumerate(zip(steps, chips)):
                sent[g, chip] = jnp.concatenate([p[j * spot_rows : (j + 1) * spot_rows] for p in picked], axis=0)
                if remote(s):
                    outward(step, g, s).start()

        in_fours(send)
        arrived[g, me] = sent[g, me]

    def tally():
        acc[...] = jnp.zeros_like(acc)

        def receive(*steps):
            chips = [behind(s) for s in steps]
            for s in steps:
                if remote(s):
                    to(0, gain_sent, gain_came, s).wait_recv()
            for chip in chips:
                here = pl.ds(pl.multiple_of(chip * spot_rows, 8), spot_rows)
                strength[chip] = gain_came[chip] * spots[2, here, :]
            force = jnp.concatenate([strength[chip] for chip in chips], axis=0)
            summed = scatter([force], spot(0, chips), spot(1, chips), surf_rows)
            acc[0:surf_rows] += summed[0:surf_rows] + summed[surf_rows:]

        in_fours(receive)
        inverse[...] = 1.0 / (1.0 + rate[...] * acc[0:surf_rows])

    def surface_all(step, g):
        acc[...] = jnp.zeros_like(acc)

        def receive(*steps):
            chips = [behind(s) for s in steps]
            for s in steps:
                if remote(s):
                    outward(step, g, s).wait_recv()
            values = [
                jnp.concatenate(
                    [arrived[g, chip, q * spot_rows : (q + 1) * spot_rows, :] * strength[chip] for chip in chips],
                    axis=0,
                )
                for q in range(mine)
            ]
            summed = scatter(values, spot(0, chips), spot(1, chips), surf_rows)
            acc[...] += summed[0 : mine * surf_rows] + summed[mine * surf_rows :]

        in_fours(receive)
        before = sea if step == 0 else sea_out
        for q in range(mine):
            here = slice(q * surf_rows, (q + 1) * surf_rows)
            there = slice((g * mine + q) * surf_rows, (g * mine + q + 1) * surf_rows)
            sea_out[there, :] = (before[there, :] + rate[...] * acc[here, :]) * inverse[...]
        table = table_of(sea_out[g * mine * surf_rows : (g + 1) * mine * surf_rows, :])

        def give_back(*steps):
            chips = [ahead(s) for s in steps]
            picked = [in_rows(p) for p in gather(table, spot(0, chips), spot(1, chips), surf_rows)]
            for j, (s, chip) in enumerate(zip(steps, chips)):
                back[g, chip] = jnp.concatenate([p[j * spot_rows : (j + 1) * spot_rows] for p in picked], axis=0)
                if remote(s):
                    homeward(step, g, s).start()

        in_fours(give_back)
        returned[g, me] = back[g, me]

    def take_all(step, g):
        flux[step, g] = jnp.zeros(flux.shape[2:], jnp.float32)

        def take_back(*steps):
            chips = [behind(s) for s in steps]
            for s in steps:
                if remote(s):
                    homeward(step, g, s).wait_recv()
            values = []
            for q in range(mine):
                here = slice(q * spot_rows, (q + 1) * spot_rows)
                values.append(
                    jnp.concatenate(
                        [(returned[g, chip, here, :] - sent[g, chip, here, :]) * flow[chip] for chip in chips], axis=0
                    )
                )
            summed = scatter(values, line_of(col_row, chips), line_of(col_lane, chips), rows)
            flux[step, g] += summed[0 : mine * rows] + summed[mine * rows :]

        in_fours(take_back)
        flux_over(step, g).start()

        def finish(s, _):
            outward(step, g, s).wait_send()
            homeward(step, g, s).wait_send()
            return 0

        lax.fori_loop(1, ring, finish, 0)

    @pl.when(upper)
    def _():
        handed.wait_send()
        lowest.wait_recv()

    for g in range(GROUPS):
        send_all(0, g)
    tally()

    @pl.when(lower)
    def _():
        for q in range(0, tracers, 2):

            def rise(i, values):
                k = levels - 2 - i
                return [parts[q + j, k] + ratios[k] * value for j, value in enumerate(values)]

            values = lax.fori_loop(0, levels - 1, rise, [parts[q + j, levels - 1] for j in range(2)], unroll=4)
            for j in range(2):
                top[piece(q + j), :] = values[j]
        top[piece(tracers), :] = lax.fori_loop(
            0, levels - 1, lambda i, value: value * ratios[levels - 2 - i], ratios[levels - 1], unroll=4
        )
        highest.start()

    for step in range(SUBSTEPS):
        for g in range(GROUPS):
            surface_all(step, g)
        for g in range(GROUPS):
            take_all(step, g)
        if step < SUBSTEPS - 1:
            for g in range(GROUPS):
                send_all(step + 1, g)

    def finish(s, _):
        to(0, gain_sent, gain_came, s).wait_send()
        return 0

    lax.fori_loop(1, ring, finish, 0)

    @pl.when(lower)
    def _():
        lowest.wait_send()
        highest.wait_send()

    @pl.when(upper)
    def _():
        highest.wait_recv()

    for g in range(GROUPS):
        here = slice(g * mine * rows, (g + 1) * mine * rows)
        flux_over(SUBSTEPS - 1, g).wait_recv()
        below[here, :] = flux[SUBSTEPS - 1, g] + flux_came[SUBSTEPS - 1, g]

    @pl.when(upper)
    def _():
        for q in range(tracers):
            below[piece(q), :] = top[piece(q), :] + top[piece(tracers), :] * below[piece(q), :]

    for step in range(SUBSTEPS):
        for g in range(GROUPS):
            flux_over(step, g).wait_send()


def forward(air, mix, scale, owner, column, coef, weight, counts, spots, sea, rate, ring, cap_rows):
    tracers, levels, _ = air.shape
    rows, surf_rows = scale.shape[0], rate.shape[0]
    mine = tracers // GROUPS
    places = 2 * ring * cap_rows
    step_rows = max(2, min(16, 2048 // places))
    while owner.shape[0] % step_rows:
        step_rows -= 2

    def real(*shape):
        return pltpu.VMEM(shape, jnp.float32)

    message = real(GROUPS, ring, mine * 2 * cap_rows, LANES)
    once = real(ring, 2 * cap_rows, LANES)
    column_state = real((tracers + 1) * rows, LANES)
    phases = 1 + 2 * SUBSTEPS * GROUPS
    return pl.pallas_call(
        functools.partial(forward_kernel, tracers, ring, cap_rows, step_rows),
        out_shape=[
            jax.ShapeDtypeStruct((tracers, levels, rows, LANES), jnp.float32),
            jax.ShapeDtypeStruct((levels, rows, LANES), jnp.float32),
            jax.ShapeDtypeStruct((tracers * rows, LANES), jnp.float32),
            jax.ShapeDtypeStruct(sea.shape, jnp.float32),
        ],
        in_specs=[HBM] * 2 + [VMEM] * 9,
        out_specs=[VMEM] * 4,
        scratch_shapes=[
            real(levels, rows, LANES),
            real(levels, rows, LANES),
            column_state,
            column_state,
            column_state,
            real(6 * places, LANES),
            real(2 * ring, LANES),
            real(4, places, LANES),
            real(2, 4, ring * cap_rows, LANES),
            pltpu.VMEM((ring, 2 * cap_rows, LANES), jnp.int32),
            pltpu.VMEM((ring, 2 * cap_rows, LANES), jnp.int32),
            once,
            once,
            once,
            once,
            real(surf_rows, LANES),
            message,
            message,
            message,
            message,
            real(SUBSTEPS, GROUPS, mine * rows, LANES),
            real(SUBSTEPS, GROUPS, mine * rows, LANES),
            real(mine * surf_rows, LANES),
            pltpu.SemaphoreType.DMA((phases, ring)),
            pltpu.SemaphoreType.DMA((phases, ring)),
            pltpu.SemaphoreType.DMA((4 + SUBSTEPS * GROUPS,)),
            pltpu.SemaphoreType.DMA((4 + SUBSTEPS * GROUPS,)),
            pltpu.SemaphoreType.DMA,
            pltpu.SemaphoreType.DMA((2, rows)),
        ],
        compiler_params=pltpu.CompilerParams(
            vmem_limit_bytes=40 * 1024 * 1024, collective_id=0, has_side_effects=True
        ),
    )(air, mix, scale, owner, column, coef, weight, counts, spots, sea, rate)


def ascend_kernel(parts, ratios, below, out, risen, sem):
    tracers, levels, rows, _ = parts.shape
    tile = 8

    def store(j):
        here = pl.ds(pl.multiple_of(j * LANES, LANES), LANES)
        return pltpu.make_async_copy(risen.at[:, :, j, :], out.at[:, :, here], sem.at[j])

    def columns(i, _):
        here = pl.ds(pl.multiple_of(i * tile, tile), tile)

        def level(n, values):
            k = levels - 1 - n
            ratio = ratios[k, here, :]
            values = [parts[q, k, here, :] + ratio * value for q, value in enumerate(values)]
            for q, value in enumerate(values):
                risen[q, k, here, :] = value
            return values

        start = [below[pl.ds(pl.multiple_of(q * rows + i * tile, tile), tile), :] for q in range(tracers)]
        lax.fori_loop(0, levels, level, start, unroll=8)

        def send(j, _):
            store(i * tile + j).start()
            return 0

        lax.fori_loop(0, tile, send, 0)
        return 0

    lax.fori_loop(0, rows // tile, columns, 0)

    def finish(j, _):
        store(j).wait()
        return 0

    lax.fori_loop(0, rows, finish, 0)


def ascend(parts, ratios, below):
    tracers, levels, rows, _ = parts.shape
    return pl.pallas_call(
        ascend_kernel,
        in_specs=[VMEM] * 3,
        out_specs=HBM,
        out_shape=jax.ShapeDtypeStruct((tracers, levels, rows * LANES), jnp.float32),
        scratch_shapes=[pltpu.VMEM(parts.shape, jnp.float32), pltpu.SemaphoreType.DMA((rows,))],
        compiler_params=pltpu.CompilerParams(vmem_limit_bytes=16 * 1024 * 1024),
    )(parts, ratios, below)


def body(
    air_state,
    mix_coef,
    flux_scale,
    sea_state,
    sea_rate,
    block_counts,
    cell_column,
    cell_owner,
    cell_coef,
    cell_weight,
    slot_cell,
    slot_frac,
):
    tracers, columns = air_state.shape[1:]
    ring = lax.axis_size("cols")
    rows = columns // BLOCK_COLS
    surf_cells = sea_state.shape[1]
    surf_rows = surf_cells // LANES
    capacity = slot_cell.shape[0] // (2 * ring)
    cap_rows = max(4, -(-capacity // LANES))

    def by_chip(values):
        values = jnp.pad(values.reshape(2, ring, capacity), ((0, 0), (0, 0), (0, cap_rows * LANES - capacity)))
        values = jnp.swapaxes(values.reshape(2, ring, cap_rows, LANES), 0, 1)
        return values.reshape(ring * 2 * cap_rows, LANES)

    cell = by_chip(slot_cell)
    spots = jnp.stack([(cell // LANES).astype(jnp.float32), (cell % LANES).astype(jnp.float32), by_chip(slot_frac)])
    parts, ratios, below, sea = forward(
        jnp.swapaxes(air_state, 0, 1),
        mix_coef,
        flux_scale.reshape(rows, LANES),
        cell_owner.reshape(-1, LANES),
        cell_column.reshape(-1, LANES),
        cell_coef.reshape(-1, LANES),
        cell_weight.reshape(-1, LANES),
        jnp.broadcast_to(block_counts.reshape(-1, 1, 1), (rows, 2, LANES)).reshape(-1, LANES),
        spots,
        sea_state.reshape(tracers * surf_rows, LANES),
        sea_rate.reshape(surf_rows, LANES),
        ring,
        cap_rows,
    )
    return (jnp.swapaxes(ascend(parts, ratios, below), 0, 1), sea.reshape(tracers, surf_cells))


def solution(mesh):
    return jax.shard_map(
        body,
        mesh=mesh,
        in_specs=(
            P("sect", None, "cols"),
            P("sect", "cols"),
            P("cols"),
            P(None, ("sect", "cols")),
            P(("sect", "cols")),
            P(("sect", "cols"), None),
            P(("sect", "cols")),
            P(("sect", "cols"), None),
            P(("sect", "cols")),
            P(("sect", "cols")),
            P(("sect", "cols")),
            P(("sect", "cols")),
        ),
        out_specs=(P("sect", None, "cols"), P(None, ("sect", "cols"))),
        check_vma=False,
    )
```

time: 107 us -> 90.5 us (0.85)
  Pallas kernels: 87.2 us -> 76.5 us
  starting transfers between devices: 3.83 us -> 0 us
  waiting for transfers between devices: 2.04 us -> 0 us
    pallas_call x5 -> x2, Pallas kernels: 87.2 us -> 76.5 us  [the longest x1 73.8 us: forward(): pl.pallas_call(functools.partial(forward_kernel, tracers, ring, cap_rows,...]
    ppermute x2 -> x0, starting transfers between devices: 3.83 us -> none  [the longest x1 2.37 us: body(): handed = lax.ppermute(descend_end(air, mix_coef), 'sect', [(0, 1)])]
    unnamed x32 -> x16, local copies, waits for them, and re-layouts: 11.3 us -> 8.1 us
    ppermute x2 -> x0, waiting for transfers between devices: 2.04 us -> none  [the longest x1 2.04 us: body(): received = lax.ppermute(ends, 'sect', [(1, 0)])]
    reshape x2, local copies, waits for them, and re-layouts: 0.18 us -> 1.85 us  [by_chip(): values.reshape(2, ring, capacity)]
  transfers between devices with their start and end apart: 2 -> 0, of which waited for: 1 -> 0; matrix products, arithmetic and copies ran while one was open for 1% -> 0% of each run, Pallas kernels for 7% -> 0%
where the time goes in v2:
time: 90.5 us; the launch traced here: 89.9 us
  Pallas kernels  76.5 us (85%)
  local copies, waits for them, and re-layouts  12.5 us (14%)
    pallas_call x1, Pallas kernels, forward(): pl.pallas_call(functools.partial(forward_kernel, tracers, ring, cap_rows,...  73.8 us
    unnamed x16, local copies, waits for them, and re-layouts  8.1 us
    pallas_call x1, Pallas kernels, ascend(): pl.pallas_call(ascend_kernel, in_specs=[VMEM] * 3, out_specs=HBM, out_sha...  2.71 us
    reshape x2, local copies, waits for them, and re-layouts, by_chip(): values.reshape(2, ring, capacity)  1.85 us

profile of v2, /device:TPU:0, one launch (start us, length us, event | category | flops | bytes accessed | tf_op | source)
XLA Modules:
  0.0 89.9 jit_solution(17925397050146633768)
XLA Ops:
  0.6 0.7 broadcast_in_dim.12
  1.4 0.1 broadcast_in_dim.13
  1.5 0.1 broadcast_in_dim.14.counts
  1.6 0.9 %reshape.160 = s32[2,16,480]{2,1,0:T(8,128)S(1)} reshape(s32[15360]{0:T(1024)} %param.22) | data formatting | bytes 122880 | tf_op jit(solution)/shard_map/reshape | solution.py:666
  2.6 0.9 %reshape.163 = f32[2,16,480]{2,1,0:T(8,128)S(1)} reshape(f32[15360]{0:T(1024)} %param.23) | data formatting | bytes 122880 | tf_op jit(solution)/shard_map/reshape | solution.py:666
  3.6 0.1 fusion
  3.6 0.9 %reshape.165.sea = f32[144,128]{1,0:T(8,128)S(1)} reshape(f32[6,3072]{1,0:T(8,128)} %param.15) | data formatting | bytes 147456 | tf_op jit(solution)/shard_map/reshape | solution.py:682
  4.6 0.0 copy-start
  4.6 2.3 %copy-done = f32[32,6,6144]{2,0,1:T(8,128)S(1)} copy-done((f32[32,6,6144]{2,0,1:T(8,128)S(1)}, f32[32,6,6144]{2,0,1:T(8,128)}, u32[]{:S(2)}) %copy-start) | copy-done | bytes 4718616
  6.9 0.0 copy-start.1
  6.9 1.1 %copy-done.1 = f32[32,6144]{1,0:T(8,128)S(1)} copy-done((f32[32,6144]{1,0:T(8,128)S(1)}, f32[32,6144]{1,0:T(8,128)}, u32[]{:S(2)}) %copy-start.1) | copy-done | bytes 786456
  8.0 0.0 copy-start.2
  8.0 0.8 copy-done.2
  8.8 0.0 copy-start.3
  8.8 0.8 copy-done.3
  9.6 0.0 copy-start.4
  9.6 0.8 copy-done.4
  10.4 0.0 copy-start.5
  10.4 0.8 copy-done.5
  11.2 0.7 copy-done.6
  12.0 0.7 copy-done.7
  12.7 73.8 %shard_map.131 = (f32[6,32,48,128]{3,2,1,0:T(8,128)S(1)}, f32[32,48,128]{2,1,0:T(8,128)S(1)}, f32[288,128]{1,0:T(8,128)S(1)}, f32[144,128]{1,0:T(8,128)S(1)}) custom-call(f32[6,32,6144]{2,1,0:T(8,128)S(1)} %bitcast.15, f32[32,6144]{1,0:T(8,128)S(1)} %copy-done.1, f32[48,128]{1,0:T(8,128)S(1)} %bitcast.20, s32[96,128]{1,0:T(8,128)S(1)} %bitcast.16, ...), custom_call_target="tpu_custom_call" | custom-call | tf_op jit(solution)/shard_map/pallas_call | solution.py:546
  86.5 2.7 %shard_map.132 = f32[6,32,6144]{2,1,0:T(8,128)} custom-call(f32[6,32,48,128]{3,2,1,0:T(8,128)S(1)} %get-tuple-element.6.parts, f32[32,48,128]{2,1,0:T(8,128)S(1)} %get-tuple-element.7.ratios, f32[288,128]{1,0:T(8,128)S(1)} %get-tuple-element.8.below), custom_call_target="tpu_custom_call" | custom-call | tf_op jit(solution)/shard_map/pallas_call | solution.py:633
  89.2 0.7 reshape.167
  (9 shorter events, 0.1 us)
Async XLA Ops:
  4.6 2.3 %copy-start = (f32[32,6,6144]{2,0,1:T(8,128)S(1)}, f32[32,6,6144]{2,0,1:T(8,128)}, u32[]{:S(2)}) copy-start(f32[32,6,6144]{2,0,1:T(8,128)} %param.12) | copy-start | bytes 14155780
  6.9 1.1 %copy-start.1 = (f32[32,6144]{1,0:T(8,128)S(1)}, f32[32,6144]{1,0:T(8,128)}, u32[]{:S(2)}) copy-start(f32[32,6144]{1,0:T(8,128)} %mix.1) | copy-start | bytes 2359300
  8.0 0.8 copy-start.2
  8.8 0.8 copy-start.3
  9.6 0.8 copy-start.4
  10.4 0.8 copy-start.5
  11.2 0.7 copy-start.6
  12.0 0.7 copy-start.7

commit v3 on v2

--- a/solution.py
+++ b/solution.py
@@ -1,4 +1,5 @@
 import functools
+import math
 
 import jax
 import jax.numpy as jnp
@@ -12,7 +13,7 @@
 SUBSTEPS = 2
 GROUPS = 2
 LANES = 128
-VMEM = pl.BlockSpec(memory_space=pltpu.VMEM)
+LIMIT = 56 * 1024 * 1024
 HBM = pl.BlockSpec(memory_space=pltpu.HBM)
 
 
@@ -66,21 +67,38 @@
     ring,
     cap_rows,
     step_rows,
+    capacity,
     air,
     mix,
-    scale,
-    owner,
-    column,
-    coef,
-    weight,
-    counts,
-    spots,
-    sea,
-    rate,
+    scale_in,
+    sea_in,
+    rate_in,
+    counts_in,
+    column_in,
+    owner_in,
+    coef_in,
+    weight_in,
+    cell_in,
+    frac_in,
+    parts_out,
+    ratios_out,
+    below_out,
+    sea_new,
     parts,
     ratios,
     below,
     sea_out,
+    scale,
+    sea,
+    rate,
+    counts,
+    column,
+    owner,
+    coef,
+    weight,
+    slot_cell,
+    slot_frac,
+    spots,
     mixes,
     inverses,
     hand,
@@ -110,6 +128,8 @@
     pair_recv,
     local_sem,
     load_sem,
+    fetch_sem,
+    store_sem,
 ):
     levels, rows = ratios.shape[0], ratios.shape[1]
     surf_rows = rate.shape[0]
@@ -207,7 +227,47 @@
             copy.wait()
         return 0
 
+    slot_rows = cell_in.shape[0]
+    first_fetches = [(counts_in, counts), (owner_in, owner), (column_in, column), (coef_in, coef), (weight_in, weight)]
+    later_fetches = [
+        (scale_in, scale),
+        (rate_in, rate),
+        (cell_in, slot_cell.at[pl.ds(0, slot_rows)]),
+        (frac_in, slot_frac.at[pl.ds(0, slot_rows)]),
+    ]
+    fetches = [
+        pltpu.make_async_copy(source, target, fetch_sem.at[i])
+        for i, (source, target) in enumerate(first_fetches + later_fetches)
+    ]
+    first_fetches, later_fetches = fetches[: len(first_fetches)], fetches[len(first_fetches) :]
+    for copy in first_fetches:
+        copy.start()
     lax.fori_loop(0, rows, start_load, 0)
+    for copy in later_fetches:
+        copy.start()
+
+    def sea_part(j):
+        here = pl.ds(pl.multiple_of(j * LANES, LANES), LANES)
+        return pltpu.make_async_copy(sea_in.at[:, here], sea.at[:, j, :], load_sem.at[2, j])
+
+    def start_sea(j, _):
+        sea_part(j).start()
+        return 0
+
+    def wait_sea(j, _):
+        sea_part(j).wait()
+        return 0
+
+    lax.fori_loop(0, surf_rows, start_sea, 0)
+    for copy in first_fetches:
+        copy.wait()
+    block_of = lax.broadcasted_iota(jnp.int32, (owner.shape[0], counts.shape[1]), 0) // 2
+    chosen = lax.broadcasted_iota(jnp.int32, (owner.shape[0], counts.shape[1]), 1) == block_of
+    live = jnp.sum(jnp.where(chosen, counts[...].astype(jnp.float32), 0.0), axis=1, keepdims=True)
+    places_in = lax.broadcasted_iota(jnp.int32, owner.shape, 1) + LANES * lax.rem(
+        lax.broadcasted_iota(jnp.int32, owner.shape, 0), 2
+    )
+    coef[...] = jnp.where(places_in.astype(jnp.float32) < live, coef[...], 0.0)
 
     places = devices * cap_rows
     blocks = step_rows * LANES // BLOCK_SLOTS
@@ -219,7 +279,6 @@
     )
     later = jnp.where(later, 1.0, 0.0).astype(jnp.bfloat16)
     numbers = lax.broadcasted_iota(jnp.int32, (step_rows, LANES), 0)
-    within = lax.rem(numbers, 2) * LANES + lax.broadcasted_iota(jnp.int32, (step_rows, LANES), 1)
 
     def sort_part(i, _):
         here = pl.ds(pl.multiple_of(i * step_rows, step_rows), step_rows)
@@ -236,7 +295,7 @@
             before = before + jnp.broadcast_to(jnp.sum(wide, axis=1, keepdims=True), before.shape)
         offset[...] = before
         rank = jnp.concatenate(ranks, axis=1).astype(jnp.int32)
-        gain = jnp.where(within < counts[here, :], coef[here, :], 0.0)
+        gain = coef[here, :]
         gain_high, gain_low = split(gain)
         flow_high, flow_low = split(weight[here, :] * gain)
         values = [
@@ -294,6 +353,7 @@
     lax.fori_loop(0, early, sort_part, 0)
     pl.semaphore_wait(barrier, ring)
     lax.fori_loop(0, rows, wait_load, 0)
+    later_fetches[0].wait()
 
     @pl.when(upper)
     def _():
@@ -333,6 +393,46 @@
         low[piece(tracers), :] = ratios[levels - 1]
         lowest.start()
 
+    stores = [
+        pltpu.make_async_copy(source, target, store_sem.at[i])
+        for i, (source, target) in enumerate(
+            [(parts, parts_out), (ratios, ratios_out), (sea_out, sea_new), (below, below_out)]
+        )
+    ]
+    stores[0].start()
+    stores[1].start()
+    for copy in later_fetches[2:]:
+        copy.wait()
+    beyond = pl.ds(slot_rows, slot_cell.shape[0] - slot_rows)
+    slot_cell[beyond, :] = jnp.zeros((slot_cell.shape[0] - slot_rows, LANES), jnp.int32)
+    slot_frac[beyond, :] = jnp.zeros((slot_cell.shape[0] - slot_rows, LANES), jnp.float32)
+    period = LANES // math.gcd(capacity, LANES)
+    lane_numbers = lax.broadcasted_iota(jnp.int32, (cap_rows, LANES), 1)
+
+    def cut(ref, row, shift):
+        window = jnp.concatenate([ref[pl.ds(row + r, 1), :] for r in range(cap_rows + 1)], axis=0)
+        if shift == 0:
+            return window[:cap_rows]
+        turned = pltpu.roll(window, LANES - shift, 1)
+        return jnp.where(lane_numbers < LANES - shift, turned[:cap_rows], turned[1:])
+
+    def place_spots(i, _):
+        for j in range(period):
+            source = i * period + j
+            row = i * (period * capacity // LANES) + j * capacity // LANES
+            cell = cut(slot_cell, row, j * capacity % LANES)
+            frac = cut(slot_frac, row, j * capacity % LANES)
+            start = lax.rem(source, ring) * spot_rows + source // ring * cap_rows
+            for r in range(cap_rows):
+                line = pl.ds(start + r, 1)
+                spots[0, line, :] = (cell[r : r + 1] // LANES).astype(jnp.float32)
+                spots[1, line, :] = lax.rem(cell[r : r + 1], LANES).astype(jnp.float32)
+                spots[2, line, :] = frac[r : r + 1]
+        return 0
+
+    lax.fori_loop(0, devices // period, place_spots, 0)
+    later_fetches[1].wait()
+    lax.fori_loop(0, surf_rows, wait_sea, 0)
     kept.wait()
     shared.wait()
 
@@ -416,11 +516,11 @@
             acc[...] += summed[0 : mine * surf_rows] + summed[mine * surf_rows :]
 
         in_fours(receive)
-        before = sea if step == 0 else sea_out
         for q in range(mine):
             here = slice(q * surf_rows, (q + 1) * surf_rows)
             there = slice((g * mine + q) * surf_rows, (g * mine + q + 1) * surf_rows)
-            sea_out[there, :] = (before[there, :] + rate[...] * acc[here, :]) * inverse[...]
+            before = sea[g * mine + q] if step == 0 else sea_out[there, :]
+            sea_out[there, :] = (before + rate[...] * acc[here, :]) * inverse[...]
         table = table_of(sea_out[g * mine * surf_rows : (g + 1) * mine * surf_rows, :])
 
         def give_back(*steps):
@@ -497,6 +597,8 @@
             for g in range(GROUPS):
                 send_all(step + 1, g)
 
+    stores[2].start()
+
     def finish(s, _):
         to(0, gain_sent, gain_came, s).wait_send()
         return 0
@@ -522,12 +624,16 @@
         for q in range(tracers):
             below[piece(q), :] = top[piece(q), :] + top[piece(tracers), :] * below[piece(q), :]
 
+    stores[3].start()
+
     for step in range(SUBSTEPS):
         for g in range(GROUPS):
             flux_over(step, g).wait_send()
-
-
-def forward(air, mix, scale, owner, column, coef, weight, counts, spots, sea, rate, ring, cap_rows):
+    for copy in stores:
+        copy.wait()
+
+
+def forward(air, mix, scale, sea, rate, counts, column, owner, coef, weight, cell, frac, ring, cap_rows, capacity):
     tracers, levels, _ = air.shape
     rows, surf_rows = scale.shape[0], rate.shape[0]
     mine = tracers // GROUPS
@@ -544,16 +650,31 @@
     column_state = real((tracers + 1) * rows, LANES)
     phases = 1 + 2 * SUBSTEPS * GROUPS
     return pl.pallas_call(
-        functools.partial(forward_kernel, tracers, ring, cap_rows, step_rows),
+        functools.partial(forward_kernel, tracers, ring, cap_rows, step_rows, capacity),
         out_shape=[
             jax.ShapeDtypeStruct((tracers, levels, rows, LANES), jnp.float32),
             jax.ShapeDtypeStruct((levels, rows, LANES), jnp.float32),
             jax.ShapeDtypeStruct((tracers * rows, LANES), jnp.float32),
-            jax.ShapeDtypeStruct(sea.shape, jnp.float32),
+            jax.ShapeDtypeStruct((tracers * surf_rows, LANES), jnp.float32),
         ],
-        in_specs=[HBM] * 2 + [VMEM] * 9,
-        out_specs=[VMEM] * 4,
+        in_specs=[HBM] * 12,
+        out_specs=[HBM] * 4,
         scratch_shapes=[
+            real(tracers, levels, rows, LANES),
+            real(levels, rows, LANES),
+            real(tracers * rows, LANES),
+            real(tracers * surf_rows, LANES),
+            real(rows, LANES),
+            real(tracers, surf_rows, LANES),
+            real(surf_rows, LANES),
+            pltpu.VMEM(counts.shape, jnp.int32),
+            pltpu.VMEM(column.shape, jnp.int32),
+            pltpu.VMEM(owner.shape, jnp.int32),
+            real(*coef.shape),
+            real(*weight.shape),
+            pltpu.VMEM((cell.shape[0] + 8, LANES), jnp.int32),
+            real(frac.shape[0] + 8, LANES),
+            real(3, ring * 2 * cap_rows, LANES),
             real(levels, rows, LANES),
             real(levels, rows, LANES),
             column_state,
@@ -582,29 +703,62 @@
             pltpu.SemaphoreType.DMA((4 + SUBSTEPS * GROUPS,)),
             pltpu.SemaphoreType.DMA((4 + SUBSTEPS * GROUPS,)),
             pltpu.SemaphoreType.DMA,
-            pltpu.SemaphoreType.DMA((2, rows)),
+            pltpu.SemaphoreType.DMA((3, rows)),
+            pltpu.SemaphoreType.DMA((9,)),
+            pltpu.SemaphoreType.DMA((4,)),
         ],
         compiler_params=pltpu.CompilerParams(
-            vmem_limit_bytes=40 * 1024 * 1024, collective_id=0, has_side_effects=True
+            vmem_limit_bytes=LIMIT, collective_id=0, has_side_effects=True
         ),
-    )(air, mix, scale, owner, column, coef, weight, counts, spots, sea, rate)
-
-
-def ascend_kernel(parts, ratios, below, out, risen, sem):
-    tracers, levels, rows, _ = parts.shape
+    )(air, mix, scale, sea, rate, counts, column, owner, coef, weight, cell, frac)
+
+
+def ascend_kernel(parts_in, ratios_in, below_in, sea, out, sea_out, risen, ratios, below, load_sem, sem, sea_sem):
+    tracers, levels, rows, _ = risen.shape
     tile = 8
+    tiles = rows // tile
+
+    def store_sea(j):
+        here = pl.ds(pl.multiple_of(j * LANES, LANES), LANES)
+        return pltpu.make_async_copy(sea.at[:, j, :], sea_out.at[:, here], sea_sem.at[j])
+
+    def start_sea(j, _):
+        store_sea(j).start()
+        return 0
+
+    def finish_sea(j, _):
+        store_sea(j).wait()
+        return 0
+
+    def load(i):
+        here = pl.ds(pl.multiple_of(i * tile, tile), tile)
+        return pltpu.make_async_copy(parts_in.at[:, :, here, :], risen.at[:, :, here, :], load_sem.at[i])
 
     def store(j):
         here = pl.ds(pl.multiple_of(j * LANES, LANES), LANES)
         return pltpu.make_async_copy(risen.at[:, :, j, :], out.at[:, :, here], sem.at[j])
 
+    firsts = [
+        pltpu.make_async_copy(ratios_in, ratios, load_sem.at[tiles]),
+        pltpu.make_async_copy(below_in, below, load_sem.at[tiles + 1]),
+    ]
+    load(0).start()
+    for copy in firsts:
+        copy.start()
+    for i in range(1, tiles):
+        load(i).start()
+    lax.fori_loop(0, sea.shape[1], start_sea, 0)
+    for copy in firsts:
+        copy.wait()
+
     def columns(i, _):
         here = pl.ds(pl.multiple_of(i * tile, tile), tile)
+        load(i).wait()
 
         def level(n, values):
             k = levels - 1 - n
             ratio = ratios[k, here, :]
-            values = [parts[q, k, here, :] + ratio * value for q, value in enumerate(values)]
+            values = [risen[q, k, here, :] + ratio * value for q, value in enumerate(values)]
             for q, value in enumerate(values):
                 risen[q, k, here, :] = value
             return values
@@ -619,25 +773,36 @@
         lax.fori_loop(0, tile, send, 0)
         return 0
 
-    lax.fori_loop(0, rows // tile, columns, 0)
+    lax.fori_loop(0, tiles, columns, 0)
 
     def finish(j, _):
         store(j).wait()
         return 0
 
     lax.fori_loop(0, rows, finish, 0)
-
-
-def ascend(parts, ratios, below):
+    lax.fori_loop(0, sea.shape[1], finish_sea, 0)
+
+
+def ascend(parts, ratios, below, sea):
     tracers, levels, rows, _ = parts.shape
     return pl.pallas_call(
         ascend_kernel,
-        in_specs=[VMEM] * 3,
-        out_specs=HBM,
-        out_shape=jax.ShapeDtypeStruct((tracers, levels, rows * LANES), jnp.float32),
-        scratch_shapes=[pltpu.VMEM(parts.shape, jnp.float32), pltpu.SemaphoreType.DMA((rows,))],
-        compiler_params=pltpu.CompilerParams(vmem_limit_bytes=16 * 1024 * 1024),
-    )(parts, ratios, below)
+        in_specs=[HBM] * 4,
+        out_specs=[HBM] * 2,
+        out_shape=[
+            jax.ShapeDtypeStruct((tracers, levels, rows * LANES), jnp.float32),
+            jax.ShapeDtypeStruct((tracers, sea.shape[1] * LANES), jnp.float32),
+        ],
+        scratch_shapes=[
+            pltpu.VMEM(parts.shape, jnp.float32),
+            pltpu.VMEM(ratios.shape, jnp.float32),
+            pltpu.VMEM(below.shape, jnp.float32),
+            pltpu.SemaphoreType.DMA((rows // 8 + 2,)),
+            pltpu.SemaphoreType.DMA((rows,)),
+            pltpu.SemaphoreType.DMA((sea.shape[1],)),
+        ],
+        compiler_params=pltpu.CompilerParams(vmem_limit_bytes=LIMIT),
+    )(parts, ratios, below, sea)
 
 
 def body(
@@ -662,29 +827,25 @@
     capacity = slot_cell.shape[0] // (2 * ring)
     cap_rows = max(4, -(-capacity // LANES))
 
-    def by_chip(values):
-        values = jnp.pad(values.reshape(2, ring, capacity), ((0, 0), (0, 0), (0, cap_rows * LANES - capacity)))
-        values = jnp.swapaxes(values.reshape(2, ring, cap_rows, LANES), 0, 1)
-        return values.reshape(ring * 2 * cap_rows, LANES)
-
-    cell = by_chip(slot_cell)
-    spots = jnp.stack([(cell // LANES).astype(jnp.float32), (cell % LANES).astype(jnp.float32), by_chip(slot_frac)])
     parts, ratios, below, sea = forward(
         jnp.swapaxes(air_state, 0, 1),
         mix_coef,
         flux_scale.reshape(rows, LANES),
+        sea_state,
+        sea_rate.reshape(surf_rows, LANES),
+        block_counts,
+        cell_column.reshape(-1, LANES),
         cell_owner.reshape(-1, LANES),
-        cell_column.reshape(-1, LANES),
         cell_coef.reshape(-1, LANES),
         cell_weight.reshape(-1, LANES),
-        jnp.broadcast_to(block_counts.reshape(-1, 1, 1), (rows, 2, LANES)).reshape(-1, LANES),
-        spots,
-        sea_state.reshape(tracers * surf_rows, LANES),
-        sea_rate.reshape(surf_rows, LANES),
+        slot_cell.reshape(-1, LANES),
+        slot_frac.reshape(-1, LANES),
         ring,
         cap_rows,
+        capacity,
     )
-    return (jnp.swapaxes(ascend(parts, ratios, below), 0, 1), sea.reshape(tracers, surf_cells))
+    air_new, sea_new = ascend(parts, ratios, below, sea.reshape(tracers, surf_rows, LANES))
+    return jnp.swapaxes(air_new, 0, 1), sea_new
 
 
 def solution(mesh):

time: 90.5 us -> 78 us (0.86)
  local copies, waits for them, and re-layouts: 12.5 us -> 0 us
    unnamed x16 -> x0, local copies, waits for them, and re-layouts: 8.1 us -> none
    reshape x8 -> x0, local copies, waits for them, and re-layouts: 3.49 us -> none  [the longest x2 1.85 us: by_chip(): values.reshape(2, ring, capacity)]
    pallas_call x1, Pallas kernels: 73.8 us -> 71.5 us  [forward(): pl.pallas_call(functools.partial(forward_kernel, tracers, ring, cap_rows,...]
    pallas_call x1, Pallas kernels: 2.71 us -> 4.95 us  [ascend(): pl.pallas_call(ascend_kernel, in_specs=[HBM] * 4, out_specs=[HBM] * 2, ou...]
    broadcast_in_dim x3 -> x0, local copies, waits for them, and re-layouts: 0.92 us -> none  [body(): jnp.broadcast_to(block_counts.reshape(-1, 1, 1), (rows, 2, LANES))]
where the time goes in v3:
time: 78 us; the launch traced here: 77.3 us
  Pallas kernels  76.5 us (98%)
  between operations  0.82 us (1%)
    pallas_call x1, Pallas kernels, forward(): pl.pallas_call(functools.partial(forward_kernel, tracers, ring, cap_rows,...  71.5 us
    pallas_call x1, Pallas kernels, ascend(): pl.pallas_call(ascend_kernel, in_specs=[HBM] * 4, out_specs=[HBM] * 2, ou...  4.95 us

profile of v3, /device:TPU:0, one launch (start us, length us, event | category | flops | bytes accessed | tf_op | source)
XLA Modules:
  0.0 77.3 jit_solution(425791967049715468)
XLA Ops:
  0.6 71.5 %shard_map.131 = (f32[6,32,48,128]{3,2,1,0:T(8,128)}, f32[32,48,128]{2,1,0:T(8,128)}, f32[288,128]{1,0:T(8,128)}, f32[144,128]{1,0:T(8,128)}) custom-call(f32[6,32,6144]{2,1,0:T(8,128)} %bitcast.11, f32[32,6144]{1,0:T(8,128)} %mix.1, f32[48,128]{1,0:T(8,128)} %bitcast.19, f32[6,3072]{1,0:T(8,128)} %sea_in.1, f32[24,128]{1,0:T(8,128)} %bitcast.20, ...), custom_call_target="tpu_custom_call" | custom-call | tf_op jit(solution)/shard_map/pallas_call | solution.py:652
  72.2 5.0 %shard_map.132 = (f32[6,32,6144]{2,1,0:T(8,128)}, f32[6,3072]{1,0:T(8,128)}) custom-call(f32[6,32,48,128]{3,2,1,0:T(8,128)} %get-tuple-element.8.parts_in, f32[32,48,128]{2,1,0:T(8,128)} %get-tuple-element.9.ratios_in, f32[288,128]{1,0:T(8,128)} %get-tuple-element.10.below_in, f32[6,24,128]{2,1,0:T(8,128)} %bitcast.12), custom_call_target="tpu_custom_call" | custom-call | tf_op jit(solution)/shard_map/pallas_call | solution.py:788

commit v4 on v3

--- a/solution.py
+++ b/solution.py
@@ -149,21 +149,38 @@
     def remote(s):
         return not (isinstance(s, int) and s == 0)
 
-    def to(phase, source, target, s):
-        return pltpu.make_async_remote_copy(
-            src_ref=source.at[ahead(s)],
-            dst_ref=target.at[me],
-            send_sem=send_sem.at[phase, s],
-            recv_sem=recv_sem.at[phase, s],
-            device_id=(sect, ahead(s)),
-            device_id_type=pl.DeviceIdType.MESH,
-        )
-
-    def outward(step, g, s):
-        return to(1 + 2 * (step * GROUPS + g), sent.at[g], arrived.at[g], s)
-
-    def homeward(step, g, s):
-        return to(2 + 2 * (step * GROUPS + g), back.at[g], returned.at[g], s)
+    class Phase:
+        def __init__(self, phase, source, target):
+            self.phase, self.source, self.target = phase, source, target
+
+        def copy(self, source, target, four, chip):
+            return pltpu.make_async_remote_copy(
+                src_ref=source,
+                dst_ref=target,
+                send_sem=send_sem.at[self.phase],
+                recv_sem=recv_sem.at[self.phase, four],
+                device_id=(sect, chip),
+                device_id_type=pl.DeviceIdType.MESH,
+            )
+
+        def start(self, four, s):
+            self.copy(self.source.at[ahead(s)], self.target.at[me], four, ahead(s)).start()
+
+        def wait_four(self, four, steps):
+            some = pl.ds(0, sum(remote(s) for s in steps))
+            self.copy(self.source.at[some], self.target.at[some], four, ahead(1)).wait_recv()
+
+        def wait_sent(self):
+            some = pl.ds(0, ring - 1)
+            self.copy(self.source.at[some], self.target.at[some], 0, ahead(1)).wait_send()
+
+    gains = Phase(0, gain_sent, gain_came)
+
+    def outward(step, g):
+        return Phase(1 + 2 * (step * GROUPS + g), sent.at[g], arrived.at[g])
+
+    def homeward(step, g):
+        return Phase(2 + 2 * (step * GROUPS + g), back.at[g], returned.at[g])
 
     def to_partner(k, source, target):
         return pltpu.make_async_remote_copy(
@@ -178,18 +195,23 @@
     def flux_over(step, g):
         return to_partner(1 + step * GROUPS + g, flux.at[step, g], flux_came.at[step, g])
 
-    def in_fours(act):
+    def in_fours(act, order=0):
         def far(i, _):
-            act(*[ring // 2 + 4 * i + j for j in range(4)])
+            act(i, *[ring // 2 + 4 * i + j for j in range(4)])
             return 0
 
         def near(i, _):
-            act(*[ring // 2 - 1 - 4 * i - j for j in range(4)])
+            act(ring // 8 + i, *[ring // 2 - 1 - 4 * i - j for j in range(4)])
             return 0
 
+        if order:
+            act(ring // 4 - 1, 3, 2, 1, 0)
+            lax.fori_loop(0, ring // 8 - 1, near, 0)
+            lax.fori_loop(0, ring // 8, far, 0)
+            return
         lax.fori_loop(0, ring // 8, far, 0)
         lax.fori_loop(0, ring // 8 - 1, near, 0)
-        act(3, 2, 1, 0)
+        act(ring // 4 - 1, 3, 2, 1, 0)
 
     def line_of(ref, chips):
         return in_line(jnp.concatenate([ref[chip] for chip in chips], axis=0))
@@ -306,10 +328,11 @@
             flow_high,
             flow_low,
         ]
-        mask = hot(own * cap_rows + rank // LANES, places)
+        mask = hot(lax.rem(own, ring) * cap_rows + rank // LANES, places // 2)
+        lane = own // ring * LANES + lax.rem(rank, LANES)
         place_acc[...] += lax.dot_general(
             jnp.concatenate([mask * in_line(value).astype(jnp.bfloat16) for value in values], axis=0),
-            hot(lax.rem(rank, LANES), LANES),
+            hot(lane, 2 * LANES),
             (((1,), (1,)), ((), ())),
             preferred_element_type=jnp.float32,
         )
@@ -368,10 +391,15 @@
         handed.start()
 
     lax.fori_loop(early, sort_steps, sort_part, 0)
-    for v in range(2):
-        sorted_cells[v] = place_acc[v * places : (v + 1) * places]
-        first = (2 + 2 * v) * places
-        sorted_cells[2 + v] = place_acc[first : first + places] + place_acc[first + places : first + 2 * places]
+    half = places // 2
+    for d in range(2):
+        rows_of, lanes_of = pl.ds(d * half, half), slice(d * LANES, (d + 1) * LANES)
+        for v in range(2):
+            sorted_cells[v, rows_of, :] = place_acc[v * half : (v + 1) * half, lanes_of]
+            first = (2 + 2 * v) * half
+            sorted_cells[2 + v, rows_of, :] = (
+                place_acc[first : first + half, lanes_of] + place_acc[first + half : first + 2 * half, lanes_of]
+            )
 
     def half_of(section):
         count = ring * cap_rows
@@ -452,11 +480,12 @@
 
     lax.fori_loop(0, ring // 2, arrange, 0)
 
-    def send_gain(s, _):
-        to(0, gain_sent, gain_came, s).start()
-        return 0
-
-    lax.fori_loop(1, ring, send_gain, 0)
+    def send_gain(four, *steps):
+        for s in steps:
+            if remote(s):
+                gains.start(four, s)
+
+    in_fours(send_gain)
     gain_came[me] = gain_sent[me]
 
     def send_all(step, g):
@@ -468,25 +497,23 @@
             bottom = bottom + jnp.concatenate([low[piece(tracers), :]] * mine, axis=0) * change
         table = table_of(bottom)
 
-        def send(*steps):
+        def send(four, *steps):
             chips = [ahead(s) for s in steps]
             picked = [in_rows(p) for p in gather(table, line_of(col_row, chips), line_of(col_lane, chips), rows)]
             for j, (s, chip) in enumerate(zip(steps, chips)):
                 sent[g, chip] = jnp.concatenate([p[j * spot_rows : (j + 1) * spot_rows] for p in picked], axis=0)
                 if remote(s):
-                    outward(step, g, s).start()
-
-        in_fours(send)
+                    outward(step, g).start(four, s)
+
+        in_fours(send, 1)
         arrived[g, me] = sent[g, me]
 
     def tally():
         acc[...] = jnp.zeros_like(acc)
 
-        def receive(*steps):
+        def receive(four, *steps):
             chips = [behind(s) for s in steps]
-            for s in steps:
-                if remote(s):
-                    to(0, gain_sent, gain_came, s).wait_recv()
+            gains.wait_four(four, steps)
             for chip in chips:
                 here = pl.ds(pl.multiple_of(chip * spot_rows, 8), spot_rows)
                 strength[chip] = gain_came[chip] * spots[2, here, :]
@@ -500,11 +527,9 @@
     def surface_all(step, g):
         acc[...] = jnp.zeros_like(acc)
 
-        def receive(*steps):
+        def receive(four, *steps):
             chips = [behind(s) for s in steps]
-            for s in steps:
-                if remote(s):
-                    outward(step, g, s).wait_recv()
+            outward(step, g).wait_four(four, steps)
             values = [
                 jnp.concatenate(
                     [arrived[g, chip, q * spot_rows : (q + 1) * spot_rows, :] * strength[chip] for chip in chips],
@@ -523,25 +548,23 @@
             sea_out[there, :] = (before + rate[...] * acc[here, :]) * inverse[...]
         table = table_of(sea_out[g * mine * surf_rows : (g + 1) * mine * surf_rows, :])
 
-        def give_back(*steps):
+        def give_back(four, *steps):
             chips = [ahead(s) for s in steps]
             picked = [in_rows(p) for p in gather(table, spot(0, chips), spot(1, chips), surf_rows)]
             for j, (s, chip) in enumerate(zip(steps, chips)):
                 back[g, chip] = jnp.concatenate([p[j * spot_rows : (j + 1) * spot_rows] for p in picked], axis=0)
                 if remote(s):
-                    homeward(step, g, s).start()
-
-        in_fours(give_back)
+                    homeward(step, g).start(four, s)
+
+        in_fours(give_back, 1)
         returned[g, me] = back[g, me]
 
     def take_all(step, g):
         flux[step, g] = jnp.zeros(flux.shape[2:], jnp.float32)
 
-        def take_back(*steps):
+        def take_back(four, *steps):
             chips = [behind(s) for s in steps]
-            for s in steps:
-                if remote(s):
-                    homeward(step, g, s).wait_recv()
+            homeward(step, g).wait_four(four, steps)
             values = []
             for q in range(mine):
                 here = slice(q * spot_rows, (q + 1) * spot_rows)
@@ -555,13 +578,8 @@
 
         in_fours(take_back)
         flux_over(step, g).start()
-
-        def finish(s, _):
-            outward(step, g, s).wait_send()
-            homeward(step, g, s).wait_send()
-            return 0
-
-        lax.fori_loop(1, ring, finish, 0)
+        outward(step, g).wait_sent()
+        homeward(step, g).wait_sent()
 
     @pl.when(upper)
     def _():
@@ -598,12 +616,7 @@
                 send_all(step + 1, g)
 
     stores[2].start()
-
-    def finish(s, _):
-        to(0, gain_sent, gain_came, s).wait_send()
-        return 0
-
-    lax.fori_loop(1, ring, finish, 0)
+    gains.wait_sent()
 
     @pl.when(lower)
     def _():
@@ -680,7 +693,7 @@
             column_state,
             column_state,
             column_state,
-            real(6 * places, LANES),
+            real(3 * places, 2 * LANES),
             real(2 * ring, LANES),
             real(4, places, LANES),
             real(2, 4, ring * cap_rows, LANES),
@@ -698,8 +711,8 @@
             real(SUBSTEPS, GROUPS, mine * rows, LANES),
             real(SUBSTEPS, GROUPS, mine * rows, LANES),
             real(mine * surf_rows, LANES),
-            pltpu.SemaphoreType.DMA((phases, ring)),
-            pltpu.SemaphoreType.DMA((phases, ring)),
+            pltpu.SemaphoreType.DMA((phases,)),
+            pltpu.SemaphoreType.DMA((phases, ring // 4)),
             pltpu.SemaphoreType.DMA((4 + SUBSTEPS * GROUPS,)),
             pltpu.SemaphoreType.DMA((4 + SUBSTEPS * GROUPS,)),
             pltpu.SemaphoreType.DMA,

time: 78 us -> 74.8 us (0.959)
  Pallas kernels: 76.5 us -> 73.2 us
    pallas_call x1, Pallas kernels: 71.5 us -> 68.3 us  [forward(): pl.pallas_call(functools.partial(forward_kernel, tracers, ring, cap_rows,...]
where the time goes in v4:
time: 74.8 us; the launch traced here: 74.1 us
  Pallas kernels  73.2 us (98%)
  between operations  0.82 us (1%)
    pallas_call x1, Pallas kernels, forward(): pl.pallas_call(functools.partial(forward_kernel, tracers, ring, cap_rows,...  68.3 us
    pallas_call x1, Pallas kernels, ascend(): pl.pallas_call(ascend_kernel, in_specs=[HBM] * 4, out_specs=[HBM] * 2, ou...  4.95 us

profile of v4, /device:TPU:0, one launch (start us, length us, event | category | flops | bytes accessed | tf_op | source)
XLA Modules:
  0.0 74.1 jit_solution(9512677880592107634)
XLA Ops:
  0.6 68.3 %shard_map.131 = (f32[6,32,48,128]{3,2,1,0:T(8,128)}, f32[32,48,128]{2,1,0:T(8,128)}, f32[288,128]{1,0:T(8,128)}, f32[144,128]{1,0:T(8,128)}) custom-call(f32[6,32,6144]{2,1,0:T(8,128)} %bitcast.11, f32[32,6144]{1,0:T(8,128)} %mix.1, f32[48,128]{1,0:T(8,128)} %bitcast.19, f32[6,3072]{1,0:T(8,128)} %sea_in.1, f32[24,128]{1,0:T(8,128)} %bitcast.20, ...), custom_call_target="tpu_custom_call" | custom-call | tf_op jit(solution)/shard_map/pallas_call | solution.py:665
  68.9 5.0 %shard_map.132 = (f32[6,32,6144]{2,1,0:T(8,128)}, f32[6,3072]{1,0:T(8,128)}) custom-call(f32[6,32,48,128]{3,2,1,0:T(8,128)} %get-tuple-element.8.parts_in, f32[32,48,128]{2,1,0:T(8,128)} %get-tuple-element.9.ratios_in, f32[288,128]{1,0:T(8,128)} %get-tuple-element.10.below_in, f32[6,24,128]{2,1,0:T(8,128)} %bitcast.12), custom_call_target="tpu_custom_call" | custom-call | tf_op jit(solution)/shard_map/pallas_call | solution.py:801

commit v5 on v4

--- a/solution.py
+++ b/solution.py
@@ -521,7 +521,7 @@
             summed = scatter([force], spot(0, chips), spot(1, chips), surf_rows)
             acc[0:surf_rows] += summed[0:surf_rows] + summed[surf_rows:]
 
-        in_fours(receive)
+        in_fours(receive, 1)
         inverse[...] = 1.0 / (1.0 + rate[...] * acc[0:surf_rows])
 
     def surface_all(step, g):
@@ -540,7 +540,7 @@
             summed = scatter(values, spot(0, chips), spot(1, chips), surf_rows)
             acc[...] += summed[0 : mine * surf_rows] + summed[mine * surf_rows :]
 
-        in_fours(receive)
+        in_fours(receive, 1)
         for q in range(mine):
             here = slice(q * surf_rows, (q + 1) * surf_rows)
             there = slice((g * mine + q) * surf_rows, (g * mine + q + 1) * surf_rows)
@@ -576,7 +576,7 @@
             summed = scatter(values, line_of(col_row, chips), line_of(col_lane, chips), rows)
             flux[step, g] += summed[0 : mine * rows] + summed[mine * rows :]
 
-        in_fours(take_back)
+        in_fours(take_back, 1)
         flux_over(step, g).start()
         outward(step, g).wait_sent()
         homeward(step, g).wait_sent()
@@ -651,7 +651,7 @@
     rows, surf_rows = scale.shape[0], rate.shape[0]
     mine = tracers // GROUPS
     places = 2 * ring * cap_rows
-    step_rows = max(2, min(16, 2048 // places))
+    step_rows = max(2, min(32, 4096 // places))
     while owner.shape[0] % step_rows:
         step_rows -= 2
 
@@ -728,7 +728,7 @@
 
 def ascend_kernel(parts_in, ratios_in, below_in, sea, out, sea_out, risen, ratios, below, load_sem, sem, sea_sem):
     tracers, levels, rows, _ = risen.shape
-    tile = 8
+    tile = 16
     tiles = rows // tile
 
     def store_sea(j):
@@ -810,7 +810,7 @@
             pltpu.VMEM(parts.shape, jnp.float32),
             pltpu.VMEM(ratios.shape, jnp.float32),
             pltpu.VMEM(below.shape, jnp.float32),
-            pltpu.SemaphoreType.DMA((rows // 8 + 2,)),
+            pltpu.SemaphoreType.DMA((rows // 16 + 2,)),
             pltpu.SemaphoreType.DMA((rows,)),
             pltpu.SemaphoreType.DMA((sea.shape[1],)),
         ],

time: 74.8 us -> 72.4 us (0.968)
  Pallas kernels: 73.2 us -> 70.9 us
    pallas_call x1, Pallas kernels: 68.3 us -> 66.1 us  [forward(): pl.pallas_call(functools.partial(forward_kernel, tracers, ring, cap_rows,...]
where the time goes in v5:
time: 72.4 us; the launch traced here: 71.7 us
  Pallas kernels  70.9 us (98%)
  between operations  0.82 us (1%)
    pallas_call x1, Pallas kernels, forward(): pl.pallas_call(functools.partial(forward_kernel, tracers, ring, cap_rows,...  66.1 us
    pallas_call x1, Pallas kernels, ascend(): pl.pallas_call(ascend_kernel, in_specs=[HBM] * 4, out_specs=[HBM] * 2, ou...  4.78 us

profile of v5, /device:TPU:0, one launch (start us, length us, event | category | flops | bytes accessed | tf_op | source)
XLA Modules:
  0.0 71.7 jit_solution(7633925217890651838)
XLA Ops:
  0.6 66.1 %shard_map.131 = (f32[6,32,48,128]{3,2,1,0:T(8,128)}, f32[32,48,128]{2,1,0:T(8,128)}, f32[288,128]{1,0:T(8,128)}, f32[144,128]{1,0:T(8,128)}) custom-call(f32[6,32,6144]{2,1,0:T(8,128)} %bitcast.11, f32[32,6144]{1,0:T(8,128)} %mix.1, f32[48,128]{1,0:T(8,128)} %bitcast.19, f32[6,3072]{1,0:T(8,128)} %sea_in.1, f32[24,128]{1,0:T(8,128)} %bitcast.20, ...), custom_call_target="tpu_custom_call" | custom-call | tf_op jit(solution)/shard_map/pallas_call | solution.py:665
  66.7 4.8 %shard_map.132 = (f32[6,32,6144]{2,1,0:T(8,128)}, f32[6,3072]{1,0:T(8,128)}) custom-call(f32[6,32,48,128]{3,2,1,0:T(8,128)} %get-tuple-element.8.parts_in, f32[32,48,128]{2,1,0:T(8,128)} %get-tuple-element.9.ratios_in, f32[288,128]{1,0:T(8,128)} %get-tuple-element.10.below_in, f32[6,24,128]{2,1,0:T(8,128)} %bitcast.12), custom_call_target="tpu_custom_call" | custom-call | tf_op jit(solution)/shard_map/pallas_call | solution.py:801
